TPU v7x, 128 devices: a whole 4x4x4 slice. The times are simulated.
128 devices in a mesh: dapw: 32 (over y, z_hi, x), dapn: 4 (over z_lo, core).
Axes of the slice: x: 4, y: 4, z: 4 (z_hi: 2, z_lo: 2; z = z_hi * 2 + z_lo), core: 2. Of those that a mesh axis runs over, the one named last changes fastest.
Arguments:
- homolog_embedding: bfloat16 [2048, 512, 256], P(('dapw', 'dapn')), may hold values from -6 to 6
- alignment_mask: int32 [2048, 512], P(('dapw', 'dapn')), may hold values 0 or 1
- pairwise_features: bfloat16 [128, 512, 512], P('dapn', 'dapw'), may hold values from -3 to 3
- residue_validity_mask: int32 [512], replicated, may hold values 0 or 1
- left_right_coefficients: bfloat16 [256, 64], replicated, may hold values from -0.375 to 0.375
- outer_output_weight: bfloat16 [1024, 128], replicated, may hold values from -1 to 1
- triangle_input_weight: bfloat16 [4, 128, 128], P(None, None, 'dapn'), may hold values from -0.5 to 0.5
- triangle_gate_weight: bfloat16 [128, 128], P(None, 'dapn'), may hold values from -0.5 to 0.5
- triangle_output_weight: bfloat16 [128, 128], replicated, may hold values from -0.5 to 0.5
Outputs:
- pair_out: bfloat16 [128, 512, 512], P('dapn', 'dapw')
All inputs are finite; a program needn't handle non-finite values. No bound on the sum of `alignment_mask` on one device may be relied on, other than what follows from the above.
Results may differ from a plain program's by a relative error of at most 0.015.
Values may be sent and summed in bfloat16 or wider, within the bound.
A program may use at most 320 MiB of HBM per device.

v0:
```python
import jax
import jax.numpy as jnp
from jax import lax
from jax.sharding import PartitionSpec as P

C_Z = 128
LATENT_WIDTH = 32


def normalize_layer(values, axis):
    center = jnp.mean(values, axis, keepdims=True)
    spread = jnp.mean(values * values, axis, keepdims=True) - center * center
    return (values - center) * lax.rsqrt(spread + 1e-05)


def outer_terms(left_cols, piece, weights, inverse_count):
    row_count = left_cols.shape[1] // LATENT_WIDTH
    col_count = piece.shape[1]
    flat_piece = piece.reshape(piece.shape[0], col_count * LATENT_WIDTH)
    outer_sum = jnp.dot(left_cols.T, flat_piece, preferred_element_type=jnp.float32) * inverse_count
    outer_sum = outer_sum.reshape(row_count, LATENT_WIDTH, col_count, LATENT_WIDTH)
    return jnp.einsum("icjd,cde->eij", outer_sum, weights, precision=lax.Precision.HIGHEST)


def body(
    homolog_embedding,
    alignment_mask,
    pairwise_features,
    residue_validity_mask,
    left_right_coefficients,
    outer_output_weight,
    triangle_input_weight,
    triangle_gate_weight,
    triangle_output_weight,
):
    sequence_rows, residue_total, input_features = homolog_embedding.shape
    channels, row_count, _ = pairwise_features.shape
    wide_count = lax.axis_size("dapw")
    narrow_count = lax.axis_size("dapn")
    own_index = lax.axis_index("dapn")
    inverse_count = 1.0 / (sequence_rows * wide_count * narrow_count)
    homolog_standardized = normalize_layer(homolog_embedding.astype(jnp.float32), 2).astype(
        jnp.bfloat16
    )
    mapped_embedding = jnp.dot(
        homolog_standardized.reshape(sequence_rows * residue_total, input_features),
        left_right_coefficients,
        preferred_element_type=jnp.float32,
    )
    mapped_embedding = mapped_embedding.reshape(
        sequence_rows, residue_total, 2 * LATENT_WIDTH
    ) * alignment_mask[:, :, None].astype(jnp.float32)
    mapped_embedding = mapped_embedding.astype(jnp.bfloat16).reshape(
        sequence_rows, residue_total * 2 * LATENT_WIDTH
    )
    out_weight = outer_output_weight.astype(jnp.float32).reshape(LATENT_WIDTH, LATENT_WIDTH, C_Z)
    regrouped = lax.all_to_all(
        mapped_embedding, ("dapw", "dapn"), split_axis=1, concat_axis=0, tiled=True
    )
    own_res = residue_total // (wide_count * narrow_count)
    regrouped = regrouped.reshape(-1, own_res, 2 * LATENT_WIDTH)
    all_seqs = regrouped.shape[0]
    left_own = regrouped[:, :, :LATENT_WIDTH].reshape(all_seqs, own_res * LATENT_WIDTH)
    right_own = regrouped[:, :, LATENT_WIDTH:]
    left_cols = lax.all_gather(left_own, "dapn", axis=1, tiled=True)
    column_means = outer_terms(
        left_cols, lax.all_gather(right_own, "dapw", axis=1, tiled=True), out_weight, inverse_count
    )
    swapped = lax.all_to_all(column_means, "dapn", split_axis=0, concat_axis=2, tiled=True)
    swapped = swapped.reshape(channels, row_count, narrow_count, wide_count, own_res)
    outer_mean = jnp.transpose(swapped, (0, 1, 3, 2, 4)).reshape(channels, row_count, residue_total)
    updated = (pairwise_features.astype(jnp.float32) + outer_mean).astype(jnp.bfloat16)
    full_pair = lax.all_gather(updated, "dapn", axis=0, tiled=True)
    normed_pair = normalize_layer(full_pair.astype(jnp.float32), 0).astype(jnp.bfloat16)
    residue_on = residue_validity_mask.astype(jnp.float32)
    row_on = lax.dynamic_slice_in_dim(residue_on, lax.axis_index("dapw") * row_count, row_count, 0)
    pair_on = row_on[:, None] * residue_on[None, :]
    projections = jnp.einsum(
        "ncd,cik->ndik", triangle_input_weight, normed_pair, preferred_element_type=jnp.float32
    )
    left_edge = (jax.nn.sigmoid(projections[0]) * projections[1] * pair_on).astype(jnp.bfloat16)
    right_edge = (jax.nn.sigmoid(projections[2]) * projections[3] * pair_on).astype(jnp.bfloat16)
    triangle = jnp.einsum(
        "cik,cjk->cij",
        left_edge,
        lax.all_gather(right_edge, "dapw", axis=1, tiled=True),
        preferred_element_type=jnp.float32,
    )
    gating = jax.nn.sigmoid(
        jnp.einsum(
            "ce,cij->eij", triangle_gate_weight, normed_pair, preferred_element_type=jnp.float32
        )
    )
    first_sum, second_sum = (
        lax.psum(jnp.sum(triangle, 0).astype(jnp.bfloat16), "dapn").astype(jnp.float32),
        lax.psum(jnp.sum(triangle * triangle, 0).astype(jnp.bfloat16), "dapn").astype(jnp.float32),
    )
    center = first_sum / C_Z
    spread = second_sum / C_Z - center * center
    triangle_normed = ((triangle - center[None]) * lax.rsqrt(spread + 1e-05)[None]).astype(
        jnp.bfloat16
    )
    weight_rows = lax.dynamic_slice_in_dim(
        triangle_output_weight, own_index * channels, channels, 0
    )
    result = lax.psum_scatter(
        jnp.einsum(
            "ce,cij->eij", weight_rows, triangle_normed, preferred_element_type=jnp.float32
        ).astype(jnp.bfloat16),
        "dapn",
        scatter_dimension=0,
        tiled=True,
    ).astype(jnp.float32)
    return (updated.astype(jnp.float32) + gating * result).astype(jnp.bfloat16)


def solution(mesh):
    return jax.shard_map(
        body,
        mesh=mesh,
        in_specs=(
            P(("dapw", "dapn"), None, None),
            P(("dapw", "dapn"), None),
            P("dapn", "dapw", None),
            P(),
            P(),
            P(),
            P(None, None, "dapn"),
            P(None, "dapn"),
            P(),
        ),
        out_specs=P("dapn", "dapw", None),
        check_vma=False,
    )
```

profile of v0, /device:TPU:1, one launch (start us, length us, event | category | flops | bytes accessed | tf_op | source)
XLA Modules:
  0.0 604.6 jit_solution(14114409417113441508)
XLA Ops:
  6.5 0.0 all-gather.5.cloned.1.call-start
  6.6 4.6 convert_reduce_fusion
  11.2 3.1 multiply_convert_fusion
  14.3 1.1 copy.57
  15.4 1.4 all_to_all.23
  16.8 0.6 copy.58
  17.4 30.6 %all_to_all.31 = bf16[16,128,256]{2,0,1:T(8,128)(2,1)S(1)} all-to-all(bf16[16,128,256]{2,0,1:T(8,128)(2,1)S(1)} %copy.58), channel_id=1, replica_groups=mesh['dapw'=32,'dapn'=4] {'dapw','dapn'}, dimensions={1} | all-to-all | bytes 2097152 | tf_op jit(solution)/shard_map/all_to_all | solution.py:57
  48.0 0.8 reshape.111
  48.9 3.1 fusion.67
  52.0 4.1 copy.59
  56.1 0.0 all-gather.5.cloned.1.call-update
  56.1 0.0 all-gather.7.cloned.1.call-start
  56.2 2.2 copy.60
  58.4 0.0 all-gather.7.cloned.1.call-update
  58.4 0.3 all-gather.9.cloned.1.call-start
  58.7 22.6 %all-gather.5.cloned.1.call-done = bf16[2048,512]{0,1:T(8,128)(2,1)} async-done(((bf16[2048,128]{0,1:T(8,128)(2,1)}), bf16[2048,512]{0,1:T(8,128)(2,1)}) %all-gather.5.cloned.1.call-update) | async-done | bytes 2097168 | tf_op jit(solution)/shard_map/all_gather | solution.py:65
  81.3 159.6 %all-gather.7.cloned.1.call-done = bf16[2048,128,32]{0,2,1:T(8,128)(2,1)} async-done(((bf16[2048,4,32]{0,2,1:T(8,128)(2,1)}), bf16[2048,128,32]{0,2,1:T(8,128)(2,1)}) %all-gather.7.cloned.1.call-update) | async-done | bytes 16777232 | tf_op jit(solution)/shard_map/all_gather | solution.py:67
  240.9 15.1 %convolution_multiply_fusion = f32[512,4096]{1,0:T(8,128)} fusion(bf16[2048,512]{0,1:T(8,128)(2,1)} %all-gather.5.cloned.1.call-done, bf16[2048,4096]{0,1:T(8,128)(2,1)} %bitcast.107), kind=kOutput, calls=%fused_computation.8 | convolution fusion | flops 8592031744 | bytes 27262976 | tf_op jit(solution)/shard_map/dot_general | solution.py:20
  256.0 20.1 %reshape.114 = f32[16,32,128,32]{3,2,1,0:T(8,128)} reshape(f32[512,4096]{1,0:T(8,128)} %convolution_multiply_fusion) | data formatting | bytes 16777216 | tf_op jit(solution)/shard_map/reshape | solution.py:21
  276.1 19.2 %convolution_bitcast_fusion.1 = f32[128,16,128]{0,2,1:T(8,128)S(1)} fusion(f32[16,32,128,32]{3,2,1,0:T(8,128)} %reshape.114, bf16[32,32,128,1]{2,1,0,3:T(8,128)(2,1)S(1)} %bitcast.101), kind=kOutput, calls=%fused_computation.26 | convolution fusion | flops 3221225472 | bytes 9699328 | tf_op jit(solution)/shard_map/icjd,cde->eij/dot_general | solution.py:22
  295.2 0.5 copy.62
  295.7 16.9 %all_to_all.32 = f32[128,16,128]{2,1,0:T(8,128)S(1)} all-to-all(f32[128,16,128]{2,1,0:T(8,128)S(1)} %copy.62), channel_id=1, replica_groups=mesh['dapw'=32,'dapn'=4] {'dapn'}, dimensions={0} | all-to-all | bytes 2097152 | tf_op jit(solution)/shard_map/all_to_all | solution.py:69
  312.7 3.0 copy.63
  315.7 4.7 copy.64
  320.4 2.9 copy.65
  323.3 1.1 add_convert_fusion
  324.4 0.0 all-gather.9.cloned.1.call-update
  324.4 0.0 all-gather.11.cloned.1.call-start
  324.5 0.1 dynamic_slice.7
  324.6 0.1 broadcast_multiply_fusion
  324.6 27.7 %all-gather.9.cloned.1.call-done = bf16[128,16,512]{2,0,1:T(8,128)(2,1)} async-done(((bf16[32,16,512]{2,0,1:T(8,128)(2,1)}), bf16[128,16,512]{2,0,1:T(8,128)(2,1)}) %all-gather.9.cloned.1.call-update) | async-done | bytes 2097168 | tf_op jit(solution)/shard_map/all_gather | solution.py:73
  352.3 2.2 convert_reduce_fusion.1
  354.6 2.4 convolution_bitcast_fusion
  357.0 1.5 fusion.53
  358.5 0.0 all-gather.11.cloned.1.call-update
  358.5 0.0 reduce-scatter.2.cloned.1.call-start
  358.6 156.7 %all-gather.11.cloned.1.call-done = bf16[32,512,512]{2,0,1:T(8,128)(2,1)} async-done(((bf16[32,16,512]{2,0,1:T(8,128)(2,1)}), bf16[32,512,512]{2,0,1:T(8,128)(2,1)}) %all-gather.11.cloned.1.call-update) | async-done | bytes 16777232 | tf_op jit(solution)/shard_map/all_gather | solution.py:86
  515.3 38.8 %fusion.66 = (bf16[16,512]{1,0:T(8,128)(2,1)S(1)}, bf16[16,512]{1,0:T(8,128)(2,1)S(1)}, f32[32,16,512]{2,1,0:T(8,128)S(1)}) fusion(bf16[32,512,512]{2,0,1:T(8,128)(2,1)} %all-gather.11.cloned.1.call-done, bf16[32,16,512]{2,0,1:T(8,128)(2,1)S(1)} %get-tuple-element.13), kind=kOutput, calls=%fused_computation.70 | convolution fusion | flops 269205504 | bytes 18382848 | tf_op jit(solution)/shard_map/cik,cjk->cij/dot_general | solution.py:83
  554.1 0.0 copy-start.11
  554.1 10.7 %all-reduce = (bf16[16,512]{1,0:T(8,128)(2,1)S(1)}, bf16[16,512]{1,0:T(8,128)(2,1)S(1)}) all-reduce(bf16[16,512]{1,0:T(8,128)(2,1)S(1)} %get-tuple-element.10, bf16[16,512]{1,0:T(8,128)(2,1)S(1)} %get-tuple-element.9), channel_id=1, replica_groups=mesh['dapw'=32,'dapn'=4] {'dapn'}, use_global_device_ids=true, to_apply=%region_7.0 | all-reduce | flops 16384 | bytes 65536 | tf_op jit(solution)/shard_map/psum | solution.py:96
  564.8 0.1 multiply_convert_fusion.1
  565.0 0.0 copy-start.5
  565.0 2.8 convolution_convert_fusion
  567.8 0.0 reduce-scatter.2.cloned.1.call-update
  567.8 0.0 copy-start.1
  567.8 26.9 %reduce-scatter.2.cloned.1.call-done = bf16[32,16,512]{2,0,1:T(8,128)(2,1)} async-done(((bf16[128,16,512]{2,0,1:T(8,128)(2,1)}), bf16[32,16,512]{2,0,1:T(8,128)(2,1)}) %reduce-scatter.2.cloned.1.call-update) | async-done | bytes 524304 | tf_op jit(solution)/shard_map/reduce_scatter | solution.py:106
  594.7 2.0 fusion.39
  596.7 1.1 copy.73
  (26 shorter events, 0.1 us)
Async XLA Ops:
  6.5 269.5 %copy-start = (bf16[1024,128]{1,0:T(8,128)(2,1)S(1)}, bf16[1024,128]{1,0:T(8,128)(2,1)}, u32[]{:S(2)}) copy-start(bf16[1024,128]{1,0:T(8,128)(2,1)} %param.14) | copy-start | bytes 786436
  6.5 4.6 copy-start.8
  6.5 4.6 copy-start.10
  6.5 74.7 %all-gather.5.cloned.1.call-start = ((), (), s32[]{:S(2)}) async-start(), calls=%async_computation.3 | async-start | bytes 2621440 | tf_op jit(solution)/shard_map/all_gather | solution.py:65
  6.5 4.6 copy-start.4
  52.0 4.2 copy-start.3
  56.1 184.8 %all-gather.7.cloned.1.call-start = ((), (), s32[]{:S(2)}) async-start(), calls=%async_computation.4 | async-start | bytes 17301504 | tf_op jit(solution)/shard_map/all_gather | solution.py:67
  58.4 293.9 %all-gather.9.cloned.1.call-start = ((), (), s32[]{:S(2)}) async-start(), calls=%async_computation.5 | async-start | bytes 2621440 | tf_op jit(solution)/shard_map/all_gather | solution.py:73
  320.4 2.9 copy-start.6
  320.4 4.1 copy-start.9
  320.4 34.2 %copy-start.7 = (bf16[4,128,32]{1,2,0:T(8,128)(2,1)S(1)}, bf16[4,128,32]{1,2,0:T(8,128)(2,1)}, u32[]{:S(2)}) copy-start(bf16[4,128,32]{1,2,0:T(8,128)(2,1)} %param.15) | copy-start | bytes 98308
  324.4 190.9 %all-gather.11.cloned.1.call-start = ((), (), s32[]{:S(2)}) async-start(), calls=%async_computation.6 | async-start | bytes 17301504 | tf_op jit(solution)/shard_map/all_gather | solution.py:86
  358.5 236.2 %reduce-scatter.2.cloned.1.call-start = ((), (), s32[]{:S(2)}) async-start(), calls=%async_computation.7 | async-start | bytes 2621440 | tf_op jit(solution)/shard_map/reduce_scatter | solution.py:106
  554.1 40.7 %copy-start.2 = (bf16[128,16,512]{2,0,1:T(8,128)(2,1)S(1)}, bf16[128,16,512]{2,0,1:T(8,128)(2,1)}, u32[]{:S(2)}) copy-start(bf16[128,16,512]{2,0,1:T(8,128)(2,1)} %all-gather.9.cloned.1.call-done) | copy-start | bytes 6291460
  554.1 40.7 %copy-start.11 = (bf16[128,32]{0,1:T(8,128)(2,1)S(1)}, bf16[128,32]{0,1:T(8,128)(2,1)}, u32[]{:S(2)}) copy-start(bf16[128,32]{0,1:T(8,128)(2,1)} %param.16) | copy-start | bytes 24580
  565.0 29.8 %copy-start.5 = (bf16[32,16,512]{2,0,1:T(8,128)(2,1)S(1)}, bf16[32,16,512]{2,0,1:T(8,128)(2,1)}, u32[]{:S(2)}) copy-start(bf16[32,16,512]{2,0,1:T(8,128)(2,1)} %add_convert_fusion) | copy-start | bytes 1572868
  567.8 30.0 %copy-start.1 = (bf16[1024,128]{1,0:T(8,128)(2,1)S(1)}, bf16[1024,128]{1,0:T(8,128)(2,1)}, u32[]{:S(2)}) copy-start(bf16[1024,128]{1,0:T(8,128)(2,1)} %param.14) | copy-start | bytes 786436
Sparse Core Ops, SparseCore 0:
  56.2 24.9 all-gather.4
  84.3 156.6 all-gather.6
  324.5 27.7 all-gather.8
  358.6 156.6 all-gather.10
  567.9 26.7 reduce-scatter.1
where the time goes:
time: 606 us; the launch traced here: 605 us
  waiting for transfers between devices  394 us (65%)
  matrix products  83.3 us (14%)
  blocking collectives  58.3 us (10%)
  local copies, waits for them, and re-layouts  45.7 us (8%)
  between operations  13.6 us (2%)
  other arithmetic  9.67 us (2%)
    all_gather x1, waiting for transfers between devices, body(): lax.all_gather(right_own, 'dapw', axis=1, tiled=True)  160 us
    all_gather x1, waiting for transfers between devices, body(): lax.all_gather(right_edge, 'dapw', axis=1, tiled=True)  157 us
    dot_general x1, matrix products, body(): jnp.einsum('cik,cjk->cij', left_edge, lax.all_gather(right_edge, 'dapw',...  38.8 us
    all_to_all x1, blocking collectives, body(): lax.all_to_all(mapped_embedding, ('dapw', 'dapn'), split_axis=1, concat_a...  30.6 us
    all_gather x1, waiting for transfers between devices, body(): full_pair = lax.all_gather(updated, 'dapn', axis=0, tiled=True)  27.7 us
    reduce_scatter x1, waiting for transfers between devices, body(): lax.psum_scatter(jnp.einsum('ce,cij->eij', weight_rows, triangle_normed,...  26.9 us
    all_gather x1, waiting for transfers between devices, body(): left_cols = lax.all_gather(left_own, 'dapn', axis=1, tiled=True)  22.6 us
    reshape x1, local copies, waits for them, and re-layouts, outer_terms(): outer_sum.reshape(row_count, LATENT_WIDTH, col_count, LATENT_WIDTH)  20.1 us
  transfers between devices with their start and end apart: 5, of which 5 were waited for; matrix products, arithmetic and copies ran while one was open for 0% of the time, Pallas kernels for 0%

commit v1 on v0

v1 whole, which is shorter than its diff:
```python
import jax
import jax.numpy as jnp
from jax import lax
from jax.experimental import pallas as pl
from jax.experimental.pallas import tpu as pltpu
from jax.sharding import PartitionSpec as P

MESH = pl.DeviceIdType.MESH
BF16, F32 = jnp.bfloat16, jnp.float32
EPS = 1e-05
SEQS = 2048
RES = 512
C_Z = 128
LAT = 32
ROWS = 16
QUADS = 4


def position():
    w, n = lax.axis_index("dapw"), lax.axis_index("dapn")
    y, zh, x = w // 8, (w // 4) % 2, w % 4
    return y, zh * 2 + n // 2, x, n % 2


def at(y, z, x, k):
    return y * 8 + (z // 2) * 4 + x, (z % 2) * 2 + k


def remote(src, dst, send, recv, device):
    return pltpu.make_async_remote_copy(
        src_ref=src, dst_ref=dst, send_sem=send, recv_sem=recv, device_id=device, device_id_type=MESH
    )


def arrived(ref, sem):
    pltpu.make_async_copy(ref, ref, sem).wait()


def signal(sem, device):
    pl.semaphore_signal(sem, inc=1, device_id=device, device_id_type=MESH)


def lanes(start, size):
    return pl.ds(pl.multiple_of(start, size), size)


def outer_kernel(
    left, right, feat, wq, w2, updated, wfull_out,
    lbuf, rbuf, lt, prod, z_opp, z_up, z_dn, in_a, in_b, in_p, in_m, own, fbuf, fwide, wfull,
    s_f, r_f, s_w, r_w, s_l1, r_l1, s_r1, r_r1, s_l2, r_l2, s_r2, r_r2, s_c, r_c, s_z, r_z,
):
    y, z, x, k = position()
    zh, zl = z // 2, z % 2
    w, n = at(y, z, x, k)
    yk = y * 2 + k
    ya, yb, yo = (y + 1) % 4, (y + 3) % 4, (y + 2) % 4
    xa, xb, xo = (x + 1) % 4, (x + 3) % 4, (x + 2) % 4
    za, zb = (z + 1) % 4, (z + 3) % 4
    row_block = y * 8 + k * 4 + z
    same = jnp.where((z == x) & (k == zh), 1, 0)

    barrier = pltpu.get_barrier_semaphore()
    for t in range(1, 8):
        o = (yk + t) % 8
        signal(barrier, at(o // 2, z, x, o % 2))
    for t in range(1, 4):
        signal(barrier, at(y, z, (x + t) % 4, k))
        signal(barrier, (w, (n + t) % 4))
    signal(barrier, at(y, za, x, k))
    signal(barrier, at(y, zb, x, k))
    for t in range(4):
        tw, tn = at(y, x, t, zh)

        @pl.when((tw != w) | (tn != n))
        def _():
            signal(barrier, (tw, tn))

        @pl.when((row_block != w) | (t != n))
        def _():
            signal(barrier, (row_block, jnp.int32(t)))

    pl.semaphore_wait(barrier, 7 + 3 + 3 + 2 + 8 - 2 * same)

    sends = []

    def push(src, dst, send, recv, device):
        copy = remote(src, dst, send, recv, device)
        copy.start()
        sends.append(copy)

    for t in range(1, 8):
        o = (yk + t) % 8
        push(left.at[:, lanes(o * 2048, 2048)], lbuf.at[x, yk], s_l1.at[t], r_l1, at(o // 2, z, x, o % 2))
    pltpu.make_async_copy(left.at[:, lanes(yk * 2048, 2048)], lbuf.at[x, yk], r_l1).start()
    for t in range(1, 4):
        o = (x + t) % 4
        push(right.at[:, :, lanes(o * 128, 128)], rbuf.at[:, x, yk], s_r1.at[t], r_r1, at(y, z, o, k))
    pltpu.make_async_copy(right.at[:, :, lanes(x * 128, 128)], rbuf.at[:, x, yk], r_r1).start()

    def feature_copy(t):
        tw, tn = at(y, x, t, zh)
        return tw, tn, remote(
            feat.at[:, :, t * 128 : (t + 1) * 128], fbuf.at[pl.ds(n * 32, 32)], s_f.at[t], r_f, (tw, tn)
        )

    for t in range(4):
        tw, tn, copy = feature_copy(t)

        @pl.when((tw != w) | (tn != n))
        def _():
            copy.start()

        @pl.when((tw == w) & (tn == n))
        def _():
            pltpu.make_async_copy(feat.at[:, :, t * 128 : (t + 1) * 128], fbuf.at[pl.ds(n * 32, 32)], r_f).start()

    for t in range(1, 4):
        push(wq, wfull.at[n], s_w.at[t], r_w, (w, (n + t) % 4))
    pltpu.make_async_copy(wq, wfull.at[n], r_w).start()

    def left_part(slab, j):
        group = (z + (2, 0, 1, 3)[j]) % 4
        return lbuf.at[slab, :, :, lanes(group * 512, 512)]

    def right_part(yy, kk, q):
        return rbuf.at[q * 8 : (q + 1) * 8, :, yy * 2 + kk]

    arrived(lbuf.at[x], r_l1)
    for j in range(QUADS):
        push(left_part(x, j), left_part(x, j), s_l2.at[0, j], r_l2.at[0, j], at(y, z, xa, k))
        push(left_part(x, j), left_part(x, j), s_l2.at[1, j], r_l2.at[1, j], at(y, z, xb, k))
    arrived(rbuf.at[:, :, yk], r_r1)
    for q in range(QUADS):
        mine = right_part(y, k, q)
        push(mine, mine, s_r2.at[0, q], r_r2.at[0, q], at(ya, z, x, k))
        push(mine, mine, s_r2.at[1, q], r_r2.at[1, q], at(yb, z, x, k))
        push(mine, mine, s_c.at[0, q], r_c.at[0, q], at(y, z, x, 1 - k))

    def product(a, q):
        def step(p, carry):
            d = q * 8 + p * 2
            pair = jnp.concatenate(
                [rbuf[d].reshape(512, 128), rbuf[d + 1].reshape(512, 128)], axis=1
            )
            value = jnp.dot(lt[a], pair, preferred_element_type=F32).astype(BF16)
            for h in range(2):
                prod[pl.ds(a * 16, 16), pl.ds(pl.multiple_of((d + h) * 32, 32), 32), :] = value[
                    :, h * 128 : (h + 1) * 128
                ].reshape(16, 32, 128)
            return carry

        lax.fori_loop(0, 4, step, 0)

    def means(a, store):
        def step(p, carry):
            i = p * 2
            pair = jnp.concatenate([prod[a * 16 + i], prod[a * 16 + i + 1]], axis=1)
            value = jnp.dot(w2[...], pair, preferred_element_type=F32) * (1.0 / SEQS)
            store(i, value[:, :128])
            store(i + 1, value[:, 128:])
            return carry

        return step

    for step in range(QUADS + 2):
        if step < QUADS:
            j = q = step
            arrived(left_part(xb, j), r_l2.at[0, j])
            if j % 2 == 0:
                push(left_part(xb, j), left_part(xb, j), s_l2.at[2, j], r_l2.at[2, j], at(y, z, xa, k))
            arrived(left_part(xa, j), r_l2.at[1, j])
            if j % 2 == 1:
                push(left_part(xa, j), left_part(xa, j), s_l2.at[2, j], r_l2.at[2, j], at(y, z, xb, k))
            for src, up in ((yb, True), (ya, False)):
                part = right_part(src, k, q)
                arrived(part, r_r2.at[0 if up else 1, q])
                if up == (q % 2 == 0):
                    push(part, part, s_r2.at[2, q], r_r2.at[2, q], at(ya if up else yb, z, x, k))
                side = 1 if up else 2
                push(part, part, s_c.at[side, q], r_c.at[side, q], at(y, z, x, 1 - k))
        if 0 <= step - 1 < QUADS:
            j = q = step - 1
            part = right_part(yo, k, q)
            arrived(part, r_r2.at[2, q])
            push(part, part, s_c.at[3, q], r_c.at[3, q], at(y, z, x, 1 - k))
            arrived(left_part(xo, j), r_l2.at[2, j])
            group = (z + (2, 0, 1, 3)[j]) % 4
            lt[j] = lbuf[:, :, :, lanes(group * 512, 512)].reshape(512, 512).T
        if 0 <= step - 2:
            q = step - 2
            for side, src in ((0, y), (1, yb), (2, ya), (3, yo)):
                arrived(right_part(src, 1 - k, q), r_c.at[side, q])
            if q < QUADS - 1:
                lax.fori_loop(0, q + 1, lambda a, c: (product(a, q), c)[1], 0)
                if q > 0:
                    lax.fori_loop(0, q, lambda b, c: (product(q, b), c)[1], 0)
                continue
            up, down = at(y, za, x, k), at(y, zb, x, k)
            product(0, q)

            def store_opp(i, value):
                z_opp[i] = value.astype(BF16)

            lax.fori_loop(0, 4, means(0, store_opp), 0)
            push(z_opp.at[0:8], in_a, s_z.at[0], r_z.at[0], up)
            lax.fori_loop(4, 8, means(0, store_opp), 0)
            push(z_opp.at[8:16], in_b, s_z.at[1], r_z.at[1], down)

            def store_own(i, value):
                own[i] = value

            product(1, q)
            lax.fori_loop(0, 8, means(1, store_own), 0)

            def store_up(i, value):
                z_up[i] = value.astype(BF16)

            def store_up_sum(i, value):
                z_up[i] = (value + in_a[i].astype(F32)).astype(BF16)

            product(2, q)
            arrived(in_a, r_z.at[0])
            lax.fori_loop(0, 4, means(2, store_up_sum), 0)
            push(z_up.at[0:8], in_p.at[0:8], s_z.at[2], r_z.at[2], up)
            lax.fori_loop(4, 8, means(2, store_up), 0)
            push(z_up.at[8:16], in_p.at[8:16], s_z.at[3], r_z.at[3], up)

            def store_down(i, value):
                z_dn[i] = value.astype(BF16)

            def store_down_sum(i, value):
                z_dn[i] = (value + in_b[i - 8].astype(F32)).astype(BF16)

            product(3, q)
            lax.fori_loop(0, 3, lambda b, c: (product(3, b), c)[1], 0)
            arrived(in_b, r_z.at[1])
            lax.fori_loop(4, 8, means(3, store_down_sum), 0)
            push(z_dn.at[8:16], in_m.at[8:16], s_z.at[4], r_z.at[4], down)
            lax.fori_loop(0, 4, means(3, store_down), 0)
            push(z_dn.at[0:8], in_m.at[0:8], s_z.at[5], r_z.at[5], down)

    arrived(fbuf, r_f)
    fwide[...] = fbuf[...].astype(F32)
    arrived(wfull, r_w)
    wfull_out[...] = wfull[...]
    arrived(in_p.at[0:8], r_z.at[2])
    arrived(in_p.at[8:16], r_z.at[3])
    arrived(in_m.at[8:16], r_z.at[4])
    arrived(in_m.at[0:8], r_z.at[5])
    for i in range(ROWS):
        total = own[i] + in_p[i].astype(F32) + in_m[i].astype(F32)
        updated[i] = (fwide[:, i, :] + total).astype(BF16)

    for copy in sends:
        copy.wait_send()
    for t in range(4):
        tw, tn, copy = feature_copy(t)

        @pl.when((tw != w) | (tn != n))
        def _():
            copy.wait_send()


def triangle_kernel(
    updated, wfull, wout, mrow, mcol, out,
    wide, gate, outgoing, edges, tri, back, tile, landed,
    s_e, r_e, s_t, r_t, s_o, r_o,
):
    y, z, x, k = position()
    w, n = at(y, z, x, k)
    me = w * 4 + n
    row_block = y * 8 + k * 4 + z

    barrier = pltpu.get_barrier_semaphore()

    def greet(t, carry):
        o = (me + t) % 128
        signal(barrier, (o // 4, o % 4))
        return carry

    lax.fori_loop(1, 128, greet, 0)

    weights = wfull[...].reshape(640, C_Z)
    col_on = mcol[pl.ds(x, 1), :]
    for i in range(ROWS):
        u = updated[i].astype(F32)
        center = jnp.sum(u, 0, keepdims=True) * (1.0 / C_Z)
        spread = jnp.sum(u * u, 0, keepdims=True) * (1.0 / C_Z) - center * center
        normed = ((u - center) * lax.rsqrt(spread + EPS)).astype(BF16)
        proj = jnp.dot(weights, normed, preferred_element_type=F32)
        on = col_on * mrow[row_block * ROWS + i].astype(F32)
        for c in range(4):
            base = c * 160
            wide[0, c * 32 : (c + 1) * 32, i, :] = (
                jax.nn.sigmoid(proj[base : base + 32]) * proj[base + 32 : base + 64] * on
            )
            wide[1, c * 32 : (c + 1) * 32, i, :] = (
                jax.nn.sigmoid(proj[base + 64 : base + 96]) * proj[base + 96 : base + 128] * on
            )
            gate[i, c * 32 : (c + 1) * 32, :] = proj[base + 128 : base + 160]
    for h in range(2):
        outgoing[:, h] = wide[h].astype(BF16)

    pl.semaphore_wait(barrier, 127)

    def send_edges(t, carry):
        o = (me + t) % 128
        remote(outgoing.at[o], edges.at[:, x, row_block], s_e, r_e, (o // 4, o % 4)).start()
        return carry

    pltpu.make_async_copy(outgoing.at[me], edges.at[:, x, row_block], r_e).start()
    lax.fori_loop(1, 128, send_edges, 0)
    gate[...] = jax.nn.sigmoid(gate[...])
    arrived(edges, r_e)

    first = jnp.concatenate([edges[0, b].reshape(RES, 128) for b in range(4)], axis=1)
    for b in range(4):
        second = jnp.concatenate(
            [edges[1, c, b * 8 : (b + 1) * 8].reshape(128, 128) for c in range(4)], axis=1
        )
        value = lax.dot_general(first, second, (((1,), (1,)), ((), ())), preferred_element_type=F32)
        tri[b] = value.astype(BF16).reshape(32, ROWS, 128)

        def send_back(t, carry):
            r = (row_block + t) % 32
            tw, tn = at(r // 8, r % 4, jnp.int32(b), (r // 4) % 2)

            @pl.when((tw != w) | (tn != n))
            def _():
                remote(tri.at[b, r], back.at[me], s_t, r_t, (tw, tn)).start()

            @pl.when((tw == w) & (tn == n))
            def _():
                pltpu.make_async_copy(tri.at[b, r], back.at[me], r_t).start()

            return carry

        lax.fori_loop(0, 32, send_back, 0)

    arrived(back, r_t)
    wide[0] = back[...].astype(F32)
    for i in range(ROWS):
        t = wide[0, :, i, :]
        center = jnp.sum(t, 0, keepdims=True) * (1.0 / C_Z)
        spread = jnp.sum(t * t, 0, keepdims=True) * (1.0 / C_Z) - center * center
        normed = ((t - center) * lax.rsqrt(spread + EPS)).astype(BF16)
        result = jnp.dot(wout[...], normed, preferred_element_type=F32)
        wide[1, :, i, :] = updated[i].astype(F32) + gate[i] * result
    tile[...] = wide[1].astype(BF16)

    def out_copy(q):
        return remote(
            tile.at[q * 32 : (q + 1) * 32],
            landed.at[:, :, lanes(x * 128, 128)],
            s_o.at[q], r_o, (row_block, jnp.int32(q)),
        )

    for q in range(4):
        away = (row_block != w) | (n != q)

        @pl.when(away)
        def _():
            out_copy(q).start()

        @pl.when(jnp.logical_not(away))
        def _():
            pltpu.make_async_copy(
                tile.at[q * 32 : (q + 1) * 32], landed.at[:, :, lanes(x * 128, 128)], r_o
            ).start()

    arrived(landed, r_o)
    out[...] = landed[...]

    arrived(outgoing.at[0:127], s_e)
    arrived(back.at[0:127], s_t)
    for q in range(4):

        @pl.when((row_block != w) | (n != q))
        def _():
            out_copy(q).wait_send()


def vmem(count):
    return [pl.BlockSpec(memory_space=pltpu.VMEM)] * count


def outer_call(left, right, feat, wq, w2):
    dma = pltpu.SemaphoreType.DMA
    return pl.pallas_call(
        outer_kernel,
        name="outer",
        out_shape=(
            jax.ShapeDtypeStruct((ROWS, C_Z, 128), BF16),
            jax.ShapeDtypeStruct((4, 160, C_Z), BF16),
        ),
        in_specs=vmem(5),
        out_specs=tuple(vmem(2)),
        scratch_shapes=[
            pltpu.VMEM((4, 8, 16, 2048), BF16),
            pltpu.VMEM((LAT, 4, 8, 16, 128), BF16),
            pltpu.VMEM((4, 512, 512), BF16),
            pltpu.VMEM((64, LAT * LAT, 128), BF16),
            pltpu.VMEM((ROWS, C_Z, 128), BF16),
            pltpu.VMEM((ROWS, C_Z, 128), BF16),
            pltpu.VMEM((ROWS, C_Z, 128), BF16),
            pltpu.VMEM((8, C_Z, 128), BF16),
            pltpu.VMEM((8, C_Z, 128), BF16),
            pltpu.VMEM((ROWS, C_Z, 128), BF16),
            pltpu.VMEM((ROWS, C_Z, 128), BF16),
            pltpu.VMEM((ROWS, C_Z, 128), F32),
            pltpu.VMEM((C_Z, ROWS, 128), BF16),
            pltpu.VMEM((C_Z, ROWS, 128), F32),
            pltpu.VMEM((4, 160, C_Z), BF16),
            dma((4,)), dma, dma((4,)), dma,
            dma((8,)), dma, dma((4,)), dma,
            dma((3, 4)), dma((3, 4)), dma((3, 4)), dma((3, 4)),
            dma((4, 4)), dma((4, 4)), dma((6,)), dma((6,)),
        ],
        compiler_params=pltpu.CompilerParams(
            collective_id=0, has_side_effects=True, vmem_limit_bytes=48 * 2**20
        ),
        cost_estimate=pl.CostEstimate(flops=11 * 10**9, bytes_accessed=3 * 2**20, transcendentals=0),
    )(left, right, feat, wq, w2)


def triangle_call(updated, wfull, wout, mrow, mcol):
    dma = pltpu.SemaphoreType.DMA
    return pl.pallas_call(
        triangle_kernel,
        name="triangle",
        out_shape=jax.ShapeDtypeStruct((32, ROWS, RES), BF16),
        in_specs=vmem(3) + [pl.BlockSpec(memory_space=pltpu.SMEM)] + vmem(1),
        out_specs=pl.BlockSpec(memory_space=pltpu.VMEM),
        scratch_shapes=[
            pltpu.VMEM((2, C_Z, ROWS, 128), F32),
            pltpu.VMEM((ROWS, C_Z, 128), F32),
            pltpu.VMEM((C_Z, 2, ROWS, 128), BF16),
            pltpu.VMEM((2, 4, 32, ROWS, 128), BF16),
            pltpu.VMEM((4, 32, ROWS, 128), BF16),
            pltpu.VMEM((C_Z, ROWS, 128), BF16),
            pltpu.VMEM((C_Z, ROWS, 128), BF16),
            pltpu.VMEM((32, ROWS, RES), BF16),
            dma, dma, dma, dma, dma((4,)), dma,
        ],
        compiler_params=pltpu.CompilerParams(
            collective_id=1, has_side_effects=True, vmem_limit_bytes=40 * 2**20
        ),
        cost_estimate=pl.CostEstimate(flops=10**9, bytes_accessed=2 * 2**20, transcendentals=10**6),
    )(updated, wfull, wout, mrow, mcol)


def body(
    homolog_embedding,
    alignment_mask,
    pairwise_features,
    residue_validity_mask,
    left_right_coefficients,
    outer_output_weight,
    triangle_input_weight,
    triangle_gate_weight,
    triangle_output_weight,
):
    seqs, residues, features = homolog_embedding.shape
    msa = homolog_embedding.astype(F32)
    center = jnp.mean(msa, 2, keepdims=True)
    spread = jnp.mean(msa * msa, 2, keepdims=True) - center * center
    normed = ((msa - center) * lax.rsqrt(spread + EPS)).astype(BF16)
    edges = jnp.dot(
        normed.reshape(seqs * residues, features),
        left_right_coefficients,
        preferred_element_type=F32,
    )
    edges = edges.reshape(seqs, residues, 2 * LAT) * alignment_mask[:, :, None].astype(F32)
    edges = edges.astype(BF16)
    left = edges[:, :, :LAT].reshape(seqs, residues * LAT)
    right = jnp.transpose(edges[:, :, LAT:], (2, 0, 1))

    w2 = jnp.transpose(outer_output_weight.reshape(LAT, LAT, C_Z), (2, 1, 0)).reshape(C_Z, LAT * LAT)
    wq = jnp.concatenate([triangle_input_weight, triangle_gate_weight[None]], 0)
    wq = jnp.transpose(wq, (0, 2, 1)).reshape(160, C_Z)
    updated, wfull = outer_call(left, right, pairwise_features, wq, w2)
    return triangle_call(
        updated, wfull, triangle_output_weight.T,
        residue_validity_mask, residue_validity_mask.astype(F32).reshape(4, 128),
    )


def solution(mesh):
    return jax.shard_map(
        body,
        mesh=mesh,
        in_specs=(
            P(("dapw", "dapn"), None, None),
            P(("dapw", "dapn"), None),
            P("dapn", "dapw", None),
            P(),
            P(),
            P(),
            P(None, None, "dapn"),
            P(None, "dapn"),
            P(),
        ),
        out_specs=P("dapn", "dapw", None),
        check_vma=False,
    )
```

time: 606 us -> 164 us (0.27)
  the two profiles are of different devices: /device:TPU:1 before, /device:TPU:33 now
where the time goes in v1:
time: 164 us
  Pallas kernels  146 us (89%)
  local copies, waits for them, and re-layouts  6.68 us (4%)
  other arithmetic  5.73 us (3%)
  matrix products  5.63 us (3%)
    pallas_call x1, Pallas kernels, outer_call(): pl.pallas_call(outer_kernel, name='outer', out_shape=(jax.ShapeDtypeStruc...  78.1 us
    pallas_call x1, Pallas kernels, triangle_call(): pl.pallas_call(triangle_kernel, name='triangle', out_shape=jax.ShapeDtype...  67.8 us
    dot_general x1, matrix products, body(): jnp.dot(normed.reshape(seqs * residues, features), left_right_coefficient...  5.63 us
    reduce_sum x1, other arithmetic, body(): center = jnp.mean(msa, 2, keepdims=True)  4.57 us
    reshape x1, local copies, waits for them, and re-layouts, body(): left = edges[:, :, :LAT].reshape(seqs, residues * LAT)  3.5 us

profile of v1, /device:TPU:33, one launch (start us, length us, event | category | flops | bytes accessed | tf_op | source)
XLA Modules:
  0.0 164.1 jit_solution(15618217557236777252)
XLA Ops:
  0.0 0.0 copy-start
  0.0 0.0 copy-start.3
  0.0 4.6 %convert_reduce_fusion = (f32[16,512]{1,0:T(8,128)S(1)}, f32[16,512]{1,0:T(8,128)S(1)}) fusion(bf16[16,512,256]{2,1,0:T(8,128)(2,1)} %param.9), kind=kLoop, calls=%fused_computation.2 | loop fusion | flops 8372224 | bytes 4259840 | tf_op jit(solution)/shard_map/reduce_sum | solution.py:465
  4.6 0.0 copy-start.5
  4.6 0.0 copy-done
  4.6 0.0 copy-done.3
  4.6 5.6 %fusion.3 = f32[16,512,64]{1,2,0:T(8,128)S(1)} fusion(bf16[16,512,256]{2,1,0:T(8,128)(2,1)S(1)} %copy-done.3, f32[16,512]{1,0:T(8,128)S(1)} %get-tuple-element.14, f32[16,512]{1,0:T(8,128)S(1)} %get-tuple-element.13, bf16[256,64]{0,1:T(8,128)(2,1)S(1)} %copy-done), kind=kOutput, calls=%fused_computation.6 | convolution fusion | flops 276824064 | bytes 6389760 | tf_op jit(solution)/shard_map/dot_general | solution.py:468
  10.3 0.0 copy-done.5
  10.3 1.1 fusion.7
  11.4 0.0 copy-start.4
  11.4 0.0 copy-start.6
  11.5 0.0 copy-start.8
  11.5 0.0 copy-start.2
  11.5 0.1 slice_bitcast_fusion
  11.6 1.9 %copy.18 = bf16[16,512,32]{2,1,0:T(8,128)(2,1)} copy(bf16[16,512,32]{1,0,2:T(8,128)(2,1)S(1)} %get-tuple-element.12) | data formatting | bytes 1048576 | tf_op jit(solution)/shard_map/slice | solution.py:475
  13.5 3.5 %reshape.39.left = bf16[16,16384]{1,0:T(8,128)(2,1)S(1)} reshape(bf16[16,512,32]{2,1,0:T(8,128)(2,1)} %copy.18) | data formatting | bytes 1048576 | tf_op jit(solution)/shard_map/reshape | solution.py:475
  17.0 0.0 copy-done.4
  17.0 0.1 copy.19
  17.1 0.1 copy.20.w2
  17.2 0.0 copy-done.6
  17.3 0.0 copy-done.8
  17.3 0.0 copy-done.2
  17.3 0.0 copy-start.7
  17.3 0.0 copy-start.1
  17.3 78.1 %outer.1 = (bf16[16,128,128]{2,1,0:T(8,128)(2,1)S(1)}, bf16[4,160,128]{2,1,0:T(8,128)(2,1)S(1)}) custom-call(bf16[16,16384]{1,0:T(8,128)(2,1)S(1)} %reshape.39.left, bf16[32,16,512]{2,1,0:T(8,128)(2,1)S(1)} %get-tuple-element.11.right, bf16[32,16,512]{2,1,0:T(8,128)(2,1)S(1)} %copy-done.2, bf16[160,128]{1,0:T(8,128)(2,1)S(1)} %bitcast.16, ...), custom_call_target="tpu_custom_call" | custom-call | flops 11000000512 | bytes 3145728 | tf_op jit(solution)/shard_map/outer/pallas_call | solution.py:389
  95.4 0.0 copy-done.7
  95.4 0.1 copy.21
  95.5 0.0 copy-done.1
  95.5 67.8 %triangle.1 = bf16[32,16,512]{2,1,0:T(8,128)(2,1)S(1)} custom-call(bf16[16,128,128]{2,1,0:T(8,128)(2,1)S(1)} %get-tuple-element.7.updated, bf16[4,160,128]{2,1,0:T(8,128)(2,1)S(1)} %get-tuple-element.8.wfull, bf16[128,128]{1,0:T(8,128)(2,1)S(1)} %bitcast.17, s32[512]{0:T(512)S(1)} %copy-done.1, f32[4,128]{1,0:T(4,128)S(1)} %convert_bitcast_fusion.mcol), custom_call_target="tpu_custom_call" | custom-call | flops 1000000000 | bytes 2097152 | tf_op jit(solution)/shard_map/triangle/pallas_call | solution.py:428
  163.3 0.8 copy.26
  (4 shorter events, 0.0 us)
Async XLA Ops:
  0.0 4.6 %copy-start = (bf16[256,64]{0,1:T(8,128)(2,1)S(1)}, bf16[256,64]{0,1:T(8,128)(2,1)}, u32[]{:S(2)}) copy-start(bf16[256,64]{0,1:T(8,128)(2,1)} %param.13) | copy-start | bytes 98308
  0.0 4.6 %copy-start.3 = (bf16[16,512,256]{2,1,0:T(8,128)(2,1)S(1)}, bf16[16,512,256]{2,1,0:T(8,128)(2,1)}, u32[]{:S(2)}) copy-start(bf16[16,512,256]{2,1,0:T(8,128)(2,1)} %param.9) | copy-start | bytes 12582916
  4.6 5.7 %copy-start.5 = (s32[16,512]{1,0:T(8,128)S(1)}, s32[16,512]{1,0:T(8,128)}, u32[]{:S(2)}) copy-start(s32[16,512]{1,0:T(8,128)} %param.10) | copy-start | bytes 98308
  11.4 5.5 %copy-start.4 = (bf16[1024,128]{1,0:T(8,128)(2,1)S(1)}, bf16[1024,128]{1,0:T(8,128)(2,1)}, u32[]{:S(2)}) copy-start(bf16[1024,128]{1,0:T(8,128)(2,1)} %param.14) | copy-start | bytes 786436
  11.4 5.8 %copy-start.6 = (bf16[4,128,32]{1,2,0:T(8,128)(2,1)S(1)}, bf16[4,128,32]{1,2,0:T(8,128)(2,1)}, u32[]{:S(2)}) copy-start(bf16[4,128,32]{1,2,0:T(8,128)(2,1)} %param.15) | copy-start | bytes 98308
  11.5 5.8 %copy-start.8 = (bf16[128,32]{0,1:T(8,128)(2,1)S(1)}, bf16[128,32]{0,1:T(8,128)(2,1)}, u32[]{:S(2)}) copy-start(bf16[128,32]{0,1:T(8,128)(2,1)} %param.16) | copy-start | bytes 24580
  11.5 5.8 %copy-start.2 = (bf16[32,16,512]{2,1,0:T(8,128)(2,1)S(1)}, bf16[32,16,512]{2,1,0:T(8,128)(2,1)}, u32[]{:S(2)}) copy-start(bf16[32,16,512]{2,1,0:T(8,128)(2,1)} %feat.1) | copy-start | bytes 1572868
  17.3 78.1 %copy-start.7 = (bf16[128,128]{1,0:T(8,128)(2,1)S(1)}, bf16[128,128]{1,0:T(8,128)(2,1)}, u32[]{:S(2)}) copy-start(bf16[128,128]{1,0:T(8,128)(2,1)} %param.17) | copy-start | bytes 98308
  17.3 78.2 %copy-start.1 = (s32[512]{0:T(512)S(1)}, s32[512]{0:T(512)}, u32[]{:S(2)}) copy-start(s32[512]{0:T(512)} %mrow.1) | copy-start | bytes 6148

commit v2 on v0

v2 whole, which is shorter than its diff:
```python
import jax
import jax.numpy as jnp
from jax import lax
from jax.experimental import pallas as pl
from jax.experimental.pallas import tpu as pltpu
from jax.sharding import PartitionSpec as P

MESH = pl.DeviceIdType.MESH
BF16, F32 = jnp.bfloat16, jnp.float32
EPS = 1e-05
SEQS = 2048
RES = 512
C_Z = 128
LAT = 32
ROWS = 16
QUADS = 4


def position():
    w, n = lax.axis_index("dapw"), lax.axis_index("dapn")
    y, zh, x = w // 8, (w // 4) % 2, w % 4
    return y, zh * 2 + n // 2, x, n % 2


def at(y, z, x, k):
    return y * 8 + (z // 2) * 4 + x, (z % 2) * 2 + k


def block_of(y, z, k):
    return y * 8 + (z // 2) * 4 + k * 2 + z % 2


def remote(src, dst, send, recv, device):
    return pltpu.make_async_remote_copy(
        src_ref=src, dst_ref=dst, send_sem=send, recv_sem=recv, device_id=device, device_id_type=MESH
    )


def arrived(ref, sem):
    pltpu.make_async_copy(ref, ref, sem).wait()


def signal(sem, device):
    pl.semaphore_signal(sem, inc=1, device_id=device, device_id_type=MESH)


def lanes(start, size):
    return pl.ds(pl.multiple_of(start, size), size)


def kernel(
    msa, msa_mask, feat, coef, w2, wq, wout, mrow, mcol, out,
    held, lwide, rwide, left, right, lbuf, rbuf, lt, prod,
    z_opp, z_up, z_dn, in_a, in_b, in_p, in_m, own, fbuf, wide, wfull,
    updated, gate, outgoing, edges, tri, back, tile, landed,
    s_x, s_f, r_f, s_w, r_w, s_l1, r_l1, s_r1, r_r1, s_l2, r_l2, s_r2, r_r2, s_c, r_c, s_z, r_z,
    s_e, r_e, s_t, r_t, s_o, r_o,
):
    y, z, x, k = position()
    feature_z, feature_k = (z // 2) * 2 + x % 2, x // 2
    w, n = at(y, z, x, k)
    me = w * 4 + n
    yk = y * 2 + k
    ya, yb, yo = (y + 1) % 4, (y + 3) % 4, (y + 2) % 4
    xa, xb, xo = (x + 1) % 4, (x + 3) % 4, (x + 2) % 4
    za, zb, zo = (z + 1) % 4, (z + 3) % 4, (z + 2) % 4
    up, down = at(y, za, x, k), at(y, zb, x, k)
    row_block = block_of(y, z, k)

    def load(g):
        part = pl.ds(g * 4, 4)
        return pltpu.make_async_copy(msa.at[part], held.at[part], s_x.at[g])

    for g in range(4):
        load(g).start()

    barrier = pltpu.get_barrier_semaphore()

    def greet(t, carry):
        o = (me + t) % 128
        signal(barrier, (o // 4, o % 4))
        return carry

    lax.fori_loop(1, 128, greet, 0)

    wl, wr = coef[:, :LAT], coef[:, LAT:]
    wide_coef = jnp.concatenate([wl] * 4 + [wr] * 4, axis=1)
    column_sum = jnp.sum(wide_coef.astype(F32), 0, keepdims=True)
    mask_columns = msa_mask[...].astype(F32).T
    lane_part = lax.broadcasted_iota(jnp.int32, (1, 128), 1) // LAT
    for g in range(4):
        load(g).wait()
        packed = jnp.zeros((RES, 128), F32)
        for h in range(4):
            s = g * 4 + h
            values = held[s]
            v = values.astype(F32)
            center = jnp.sum(v, 1, keepdims=True) * (1.0 / 256)
            spread = jnp.sum(v * v, 1, keepdims=True) * (1.0 / 256) - center * center
            scale = lax.rsqrt(spread + EPS) * mask_columns[:, s : s + 1]
            mapped = jnp.dot(values, wide_coef, preferred_element_type=F32)
            mapped = (mapped - center * column_sum) * scale
            lefts = mapped[:, :128].reshape(16, 4, 8, 128)
            merged = lefts[:, 0]
            for rr in range(1, 4):
                merged = jnp.where(lane_part[None] == rr, lefts[:, rr], merged)
            lwide[s] = merged.reshape(128, 128)
            packed = jnp.where(lane_part == h, mapped[:, 128:], packed)
        rwide[g * 4 : (g + 1) * 4] = packed.T.reshape(4, LAT, RES)
    for t in range(128):
        left[:, t * 128 : (t + 1) * 128] = lwide[:, t, :].astype(BF16)
    for d in range(LAT):
        right[d] = rwide[:, d, :].astype(BF16)

    pl.semaphore_wait(barrier, 127)

    sends = []

    def push(src, dst, send, recv, device):
        copy = remote(src, dst, send, recv, device)
        copy.start()
        sends.append(copy)

    def left_block(o, h):
        return left.at[:, lanes((o // 2) * 4096 + h * 2048 + (o % 2) * 1024, 1024)]

    for h in range(2):
        target = lbuf.at[x, yk, :, h * 1024 : (h + 1) * 1024]
        for t in range(1, 8):
            o = (yk + t) % 8
            push(left_block(o, h), target, s_l1.at[h, t], r_l1, at(o // 2, z, x, o % 2))
        pltpu.make_async_copy(left_block(yk, h), target, r_l1).start()
    for t in range(1, 4):
        o = (x + t) % 4
        push(right.at[:, :, lanes(o * 128, 128)], rbuf.at[:, x, yk], s_r1.at[t], r_r1, at(y, z, o, k))
    pltpu.make_async_copy(right.at[:, :, lanes(x * 128, 128)], rbuf.at[:, x, yk], r_r1).start()

    for t in range(1, 4):
        push(wq, wfull.at[n], s_w.at[t], r_w, (w, (n + t) % 4))
    pltpu.make_async_copy(wq, wfull.at[n], r_w).start()

    def feature_copy(t):
        tw, tn = at(y, feature_z, t, feature_k)
        return tw, tn, remote(
            feat.at[:, :, t * 128 : (t + 1) * 128], fbuf.at[pl.ds(n * 32, 32)], s_f.at[t], r_f, (tw, tn)
        )

    def half_of(p):
        return (z // 2 + 1 + p // 2) % 2

    def left_part(slab, p):
        return lbuf.at[slab, (p % 2) * 4 : (p % 2) * 4 + 4, :, lanes(half_of(p) * 1024, 1024)]

    def right_part(yy, kk, q):
        return rbuf.at[q * 8 : (q + 1) * 8, :, yy * 2 + kk]

    arrived(lbuf.at[x], r_l1)
    for p in range(QUADS):
        push(left_part(x, p), left_part(x, p), s_l2.at[0, p], r_l2.at[0, p], at(y, z, xa, k))
        push(left_part(x, p), left_part(x, p), s_l2.at[1, p], r_l2.at[1, p], at(y, z, xb, k))
    arrived(rbuf.at[:, :, yk], r_r1)
    for q in range(QUADS):
        mine = right_part(y, k, q)
        push(mine, mine, s_r2.at[0, q], r_r2.at[0, q], at(ya, z, x, k))
        push(mine, mine, s_r2.at[1, q], r_r2.at[1, q], at(yb, z, x, k))
        push(mine, mine, s_c.at[0, q], r_c.at[0, q], at(y, z, x, 1 - k))

    def product(a, q):
        parts = [rbuf[q * 8 + h].reshape(512, 128) for h in range(8)]
        value = jnp.dot(lt[a], jnp.concatenate(parts, axis=1), preferred_element_type=F32).astype(BF16)
        for h in range(8):
            prod[pl.ds(a * 16, 16), pl.ds(pl.multiple_of((q * 8 + h) * 32, 32), 32), :] = value[
                :, h * 128 : (h + 1) * 128
            ].reshape(16, 32, 128)

    def products(half, first, last):
        def step(t, carry):
            product(half * 2 + t % 2, first + t // 2)
            return carry

        lax.fori_loop(0, (last - first) * 2, step, 0)

    def means(a, part, store):
        rows = [prod[a * 16 + part * 8 + h] for h in range(8)]
        value = jnp.dot(w2[...], jnp.concatenate(rows, axis=1), preferred_element_type=F32) * (1.0 / SEQS)
        for h in range(8):
            store(part * 8 + h, value[:, h * 128 : (h + 1) * 128])

    for step in range(QUADS + 2):
        if step < QUADS:
            p = q = step
            for src, upward in ((yb, True), (ya, False)):
                part = right_part(src, k, q)
                arrived(part, r_r2.at[0 if upward else 1, q])
                if upward == (q % 2 == 0):
                    push(part, part, s_r2.at[2, q], r_r2.at[2, q], at(ya if upward else yb, z, x, k))
                side = 1 if upward else 2
                push(part, part, s_c.at[side, q], r_c.at[side, q], at(y, z, x, 1 - k))
            for src, upward in ((xb, True), (xa, False)):
                part = left_part(src, p)
                arrived(part, r_l2.at[0 if upward else 1, p])
                if upward == (p % 2 == 0):
                    push(part, part, s_l2.at[2, p], r_l2.at[2, p], at(y, z, xa if upward else xb, k))
        if 0 <= step - 1 < QUADS:
            p = q = step - 1
            part = right_part(yo, k, q)
            arrived(part, r_r2.at[2, q])
            push(part, part, s_c.at[3, q], r_c.at[3, q], at(y, z, x, 1 - k))
            arrived(left_part(xo, p), r_l2.at[2, p])
            if p % 2 == 1:
                half = half_of(p)
                turned = lbuf[:, :, :, lanes(half * 1024, 1024)].reshape(512, 1024).T
                for m in range(32):
                    zl, i = m // 16, m % 16
                    row = ((i % 8) * 4 + zl * 2 + i // 8) * 32
                    lt[half * 2 + zl, i * 32 : (i + 1) * 32] = turned[row : row + 32]
        if 0 <= step - 2:
            q = step - 2
            for side, src in ((0, y), (1, yb), (2, ya), (3, yo)):
                arrived(right_part(src, 1 - k, q), r_c.at[side, q])
            if q < QUADS - 1:
                products(half_of(0), q, q + 1)
                if q == QUADS - 2:
                    products(half_of(2), 0, q + 1)

    for t in range(4):
        tw, tn, copy = feature_copy(t)

        @pl.when((tw != w) | (tn != n))
        def _():
            copy.start()

        @pl.when((tw == w) & (tn == n))
        def _():
            pltpu.make_async_copy(feat.at[:, :, t * 128 : (t + 1) * 128], fbuf.at[pl.ds(n * 32, 32)], r_f).start()

    def store_opp(i, value):
        z_opp[i] = value.astype(BF16)

    def store_own(i, value):
        own[i] = value

    def store_up(i, value):
        z_up[i] = value.astype(BF16)

    def store_up_sum(i, value):
        z_up[i] = (value + in_a[i].astype(F32)).astype(BF16)

    def store_down(i, value):
        z_dn[i] = value.astype(BF16)

    def store_down_sum(i, value):
        z_dn[i] = (value + in_b[i - 8].astype(F32)).astype(BF16)

    product(zo, 3)
    means(zo, 0, store_opp)
    push(z_opp.at[0:8], in_a, s_z.at[0], r_z.at[0], up)
    means(zo, 1, store_opp)
    push(z_opp.at[8:16], in_b, s_z.at[1], r_z.at[1], down)
    product(za, 3)
    means(za, 1, store_up)
    push(z_up.at[8:16], in_p.at[8:16], s_z.at[3], r_z.at[3], up)
    product(zb, 3)
    means(zb, 0, store_down)
    push(z_dn.at[0:8], in_m.at[0:8], s_z.at[5], r_z.at[5], down)
    arrived(in_a, r_z.at[0])
    means(za, 0, store_up_sum)
    push(z_up.at[0:8], in_p.at[0:8], s_z.at[2], r_z.at[2], up)
    arrived(in_b, r_z.at[1])
    means(zb, 1, store_down_sum)
    push(z_dn.at[8:16], in_m.at[8:16], s_z.at[4], r_z.at[4], down)
    product(z, 3)
    for part in range(2):
        means(z, part, store_own)

    arrived(fbuf, r_f)
    wide[0] = fbuf[...].astype(F32)
    arrived(wfull, r_w)
    weights = wfull[...].reshape(640, C_Z)
    col_on = mcol[pl.ds(x, 1), :]
    arrived(in_p.at[8:16], r_z.at[3])
    arrived(in_m.at[0:8], r_z.at[5])
    arrived(in_p.at[0:8], r_z.at[2])
    arrived(in_m.at[8:16], r_z.at[4])
    for i in range(ROWS):
        total = own[i] + in_p[i].astype(F32) + in_m[i].astype(F32)
        updated[i] = (wide[0, :, i, :] + total).astype(BF16)
    for i in range(ROWS):
        u = updated[i].astype(F32)
        center = jnp.sum(u, 0, keepdims=True) * (1.0 / C_Z)
        spread = jnp.sum(u * u, 0, keepdims=True) * (1.0 / C_Z) - center * center
        normed = ((u - center) * lax.rsqrt(spread + EPS)).astype(BF16)
        proj = jnp.dot(weights, normed, preferred_element_type=F32)
        on = col_on * mrow[row_block * ROWS + i].astype(F32)
        for c in range(4):
            base = c * 160
            wide[0, c * 32 : (c + 1) * 32, i, :] = (
                jax.nn.sigmoid(proj[base : base + 32]) * proj[base + 32 : base + 64] * on
            )
            wide[1, c * 32 : (c + 1) * 32, i, :] = (
                jax.nn.sigmoid(proj[base + 64 : base + 96]) * proj[base + 96 : base + 128] * on
            )
            gate[i, c * 32 : (c + 1) * 32, :] = proj[base + 128 : base + 160]
    for h in range(2):
        outgoing[:, h] = wide[h].astype(BF16)

    def send_edges(t, carry):
        o = (me + t * 37) % 128
        remote(outgoing.at[o], edges.at[:, x, row_block], s_e, r_e, (o // 4, o % 4)).start()
        return carry

    pltpu.make_async_copy(outgoing.at[me], edges.at[:, x, row_block], r_e).start()
    lax.fori_loop(1, 128, send_edges, 0)
    gate[...] = jax.nn.sigmoid(gate[...])
    arrived(edges, r_e)

    first = jnp.concatenate([edges[0, b].reshape(RES, 128) for b in range(4)], axis=1)
    for q in (1, 3, 2, 0):
        b = (x + q) % 4
        second = jnp.concatenate(
            [edges[1, c, pl.ds(b * 8, 8)].reshape(128, 128) for c in range(4)], axis=1
        )
        value = lax.dot_general(first, second, (((1,), (1,)), ((), ())), preferred_element_type=F32)
        tri[b] = value.astype(BF16).reshape(32, ROWS, 128)

        def send_back(t, carry):
            r = (row_block + t * 11) % 32
            tw, tn = at(r // 8, ((r // 4) % 2) * 2 + r % 2, b, (r // 2) % 2)

            @pl.when((tw != w) | (tn != n))
            def _():
                remote(tri.at[b, r], back.at[me], s_t, r_t, (tw, tn)).start()

            @pl.when((tw == w) & (tn == n))
            def _():
                pltpu.make_async_copy(tri.at[b, r], back.at[me], r_t).start()

            return carry

        lax.fori_loop(0, 32, send_back, 0)

    arrived(back, r_t)
    wide[0] = back[...].astype(F32)
    for i in range(ROWS):
        t = wide[0, :, i, :]
        center = jnp.sum(t, 0, keepdims=True) * (1.0 / C_Z)
        spread = jnp.sum(t * t, 0, keepdims=True) * (1.0 / C_Z) - center * center
        normed = ((t - center) * lax.rsqrt(spread + EPS)).astype(BF16)
        result = jnp.dot(wout[...], normed, preferred_element_type=F32)
        wide[1, :, i, :] = updated[i].astype(F32) + gate[i] * result
    tile[...] = wide[1].astype(BF16)

    def out_parts(t):
        q = (x + t) % 4
        part = tile.at[pl.ds(q * 32, 32)]
        place = landed.at[:, :, lanes(x * 128, 128)]
        away = (row_block != w) | (n != q)
        return away, part, place, remote(part, place, s_o.at[t], r_o, (row_block, q))

    for t in range(4):
        away, part, place, copy = out_parts(t)

        @pl.when(away)
        def _():
            copy.start()

        @pl.when(jnp.logical_not(away))
        def _():
            pltpu.make_async_copy(part, place, r_o).start()

    arrived(landed, r_o)
    out[...] = landed[...]

    arrived(outgoing.at[0:127], s_e)
    arrived(back.at[0:127], s_t)
    for t in range(4):
        away, part, place, copy = out_parts(t)

        @pl.when(away)
        def _():
            copy.wait_send()

    for copy in sends:
        copy.wait_send()
    for t in range(4):
        tw, tn, copy = feature_copy(t)

        @pl.when((tw != w) | (tn != n))
        def _():
            copy.wait_send()


def call(msa, msa_mask, feat, coef, w2, wq, wout, mrow, mcol):
    dma = pltpu.SemaphoreType.DMA
    vmem = pl.BlockSpec(memory_space=pltpu.VMEM)
    pair = pltpu.VMEM((ROWS, C_Z, 128), BF16)
    return pl.pallas_call(
        kernel,
        name="evoformer",
        out_shape=jax.ShapeDtypeStruct((32, ROWS, RES), BF16),
        in_specs=[pl.BlockSpec(memory_space=pl.ANY)]
        + [vmem] * 6
        + [pl.BlockSpec(memory_space=pltpu.SMEM), vmem],
        out_specs=vmem,
        scratch_shapes=[
            pltpu.VMEM((16, RES, 256), BF16),
            pltpu.VMEM((16, 128, 128), F32),
            pltpu.VMEM((16, LAT, RES), F32),
            pltpu.VMEM((16, RES * LAT), BF16),
            pltpu.VMEM((LAT, 16, RES), BF16),
            pltpu.VMEM((4, 8, 16, 2048), BF16),
            pltpu.VMEM((LAT, 4, 8, 16, 128), BF16),
            pltpu.VMEM((4, 512, 512), BF16),
            pltpu.VMEM((64, LAT * LAT, 128), BF16),
            pair, pair, pair,
            pltpu.VMEM((8, C_Z, 128), BF16),
            pltpu.VMEM((8, C_Z, 128), BF16),
            pair, pair,
            pltpu.VMEM((ROWS, C_Z, 128), F32),
            pltpu.VMEM((C_Z, ROWS, 128), BF16),
            pltpu.VMEM((2, C_Z, ROWS, 128), F32),
            pltpu.VMEM((4, 160, C_Z), BF16),
            pair,
            pltpu.VMEM((ROWS, C_Z, 128), F32),
            pltpu.VMEM((C_Z, 2, ROWS, 128), BF16),
            pltpu.VMEM((2, 4, 32, ROWS, 128), BF16),
            pltpu.VMEM((4, 32, ROWS, 128), BF16),
            pltpu.VMEM((C_Z, ROWS, 128), BF16),
            pltpu.VMEM((C_Z, ROWS, 128), BF16),
            pltpu.VMEM((32, ROWS, RES), BF16),
            dma((4,)),
            dma((4,)), dma, dma((4,)), dma,
            dma((2, 8)), dma, dma((4,)), dma,
            dma((3, 4)), dma((3, 4)), dma((3, 4)), dma((3, 4)),
            dma((4, 4)), dma((4, 4)), dma((6,)), dma((6,)),
            dma, dma, dma, dma, dma((4,)), dma,
        ],
        compiler_params=pltpu.CompilerParams(
            collective_id=0, has_side_effects=True, vmem_limit_bytes=56 * 2**20
        ),
        cost_estimate=pl.CostEstimate(flops=12 * 10**9, bytes_accessed=8 * 2**20, transcendentals=10**6),
    )(msa, msa_mask, feat, coef, w2, wq, wout, mrow, mcol)


def body(
    homolog_embedding,
    alignment_mask,
    pairwise_features,
    residue_validity_mask,
    left_right_coefficients,
    outer_output_weight,
    triangle_input_weight,
    triangle_gate_weight,
    triangle_output_weight,
):
    w2 = jnp.transpose(outer_output_weight.reshape(LAT, LAT, C_Z), (2, 1, 0)).reshape(C_Z, LAT * LAT)
    wq = jnp.concatenate([triangle_input_weight, triangle_gate_weight[None]], 0)
    wq = jnp.transpose(wq, (0, 2, 1)).reshape(160, C_Z)
    return call(
        homolog_embedding, alignment_mask, pairwise_features, left_right_coefficients,
        w2, wq, triangle_output_weight.T,
        residue_validity_mask, residue_validity_mask.astype(F32).reshape(4, 128),
    )


def solution(mesh):
    return jax.shard_map(
        body,
        mesh=mesh,
        in_specs=(
            P(("dapw", "dapn"), None, None),
            P(("dapw", "dapn"), None),
            P("dapn", "dapw", None),
            P(),
            P(),
            P(),
            P(None, None, "dapn"),
            P(None, "dapn"),
            P(),
        ),
        out_specs=P("dapn", "dapw", None),
        check_vma=False,
    )
```

time: 606 us -> 139 us (0.23)
  waiting for transfers between devices: 394 us -> 0 us
  Pallas kernels: 0 us -> 129 us
  matrix products: 83.3 us -> 0 us
  blocking collectives: 58.3 us -> 0 us
  local copies, waits for them, and re-layouts: 45.7 us -> 6.73 us
  between operations: 13.6 us -> 0.01 us
  other arithmetic: 9.67 us -> 2.64 us
    all_gather x4 -> x0, waiting for transfers between devices: 367 us -> none  [the longest x1 160 us: body(): lax.all_gather(right_own, 'dapw', axis=1, tiled=True)]
    pallas_call x0 -> x1, Pallas kernels: none -> 129 us  [call(): pl.pallas_call(kernel, name='evoformer', out_shape=jax.ShapeDtypeStruct((...]
    dot_general x7 -> x0, matrix products: 83.3 us -> none  [the longest x1 38.8 us: body(): jnp.einsum('cik,cjk->cij', left_edge, lax.all_gather(right_edge, 'dapw',...]
    all_to_all x2 -> x0, blocking collectives: 47.6 us -> none  [the longest x1 30.6 us: body(): lax.all_to_all(mapped_embedding, ('dapw', 'dapn'), split_axis=1, concat_a...]
    reduce_scatter x1 -> x0, waiting for transfers between devices: 26.9 us -> none  [body(): lax.psum_scatter(jnp.einsum('ce,cij->eij', weight_rows, triangle_normed,...]
    reshape x3 -> x1, local copies, waits for them, and re-layouts: 23.8 us -> 0.85 us  [body(): jnp.transpose(outer_output_weight.reshape(LAT, LAT, C_Z), (2, 1, 0))]
    psum x1 -> x0, blocking collectives: 10.7 us -> none  [body(): lax.psum(jnp.sum(triangle * triangle, 0).astype(jnp.bfloat16), 'dapn')]
    slice x3 -> x0, local copies, waits for them, and re-layouts: 9.43 us -> none  [the longest x2 5.36 us: body(): right_own = regrouped[:, :, LATENT_WIDTH:]]
  transfers between devices with their start and end apart: 5 -> 0, of which waited for: 5 -> 0; matrix products, arithmetic and copies ran while one was open for 0% -> 0% of each run, Pallas kernels for 0% -> 0%
where the time goes in v2:
time: 139 us; the launch traced here: 138 us
  Pallas kernels  129 us (93%)
  local copies, waits for them, and re-layouts  6.73 us (5%)
  other arithmetic  2.64 us (2%)
    pallas_call x1, Pallas kernels, call(): pl.pallas_call(kernel, name='evoformer', out_shape=jax.ShapeDtypeStruct((...  129 us
    unnamed x3, local copies, waits for them, and re-layouts  4.82 us

profile of v2, /device:TPU:1, one launch (start us, length us, event | category | flops | bytes accessed | tf_op | source)
XLA Modules:
  0.0 137.9 jit_solution(9741757739071232001)
XLA Ops:
  0.0 1.3 convert_bitcast_fusion.mcol
  1.3 1.5 %copy.17 = bf16[128,128]{0,1:T(8,128)(2,1)} copy(bf16[128,128]{1,0:T(8,128)(2,1)} %param.17) | data formatting | bytes 65536 | tf_op args[8]
  2.7 1.4 pad_maximum_fusion
  4.1 1.5 %copy.18.coef = bf16[256,64]{1,0:T(8,128)(2,1)} copy(bf16[256,64]{0,1:T(8,128)(2,1)} %param.13) | data formatting | bytes 65536 | tf_op args[4]
  5.6 1.1 copy.16
  6.6 0.9 copy.19.w2
  7.5 128.6 %evoformer.1 = bf16[32,16,512]{2,1,0:T(8,128)(2,1)} custom-call(bf16[16,512,256]{2,1,0:T(8,128)(2,1)} %msa.1, s32[16,512]{1,0:T(8,128)} %msa_mask.1, bf16[32,16,512]{2,1,0:T(8,128)(2,1)} %feat.1, bf16[256,64]{1,0:T(8,128)(2,1)} %copy.18.coef, bf16[128,1024]{1,0:T(8,128)(2,1)} %copy.19.w2, bf16[160,128]{1,0:T(8,128)(2,1)} %bitcast.13, ...), custom_call_target="tpu_custom_call" | custom-call | flops 12000000000 | bytes 8388608 | tf_op jit(solution)/shard_map/evoformer/pallas_call | solution.py:397
  136.1 1.9 %copy.21 = bf16[32,16,512]{2,1,0:T(8,128)(2,1)} copy(bf16[32,16,512]{2,1,0:T(8,128)(2,1)} %evoformer.1) | data formatting | bytes 1048576

commit v3 on v2

--- a/solution.py
+++ b/solution.py
@@ -49,12 +49,12 @@
 
 
 def kernel(
-    msa, msa_mask, feat, coef, w2, wq, wout, mrow, mcol, out,
-    held, lwide, rwide, left, right, lbuf, rbuf, lt, prod,
-    z_opp, z_up, z_dn, in_a, in_b, in_p, in_m, own, fbuf, wide, wfull,
-    updated, gate, outgoing, edges, tri, back, tile, landed,
-    s_x, s_f, r_f, s_w, r_w, s_l1, r_l1, s_r1, r_r1, s_l2, r_l2, s_r2, r_r2, s_c, r_c, s_z, r_z,
-    s_e, r_e, s_t, r_t, s_o, r_o,
+    msa, msa_mask, feat, coef, w_outer, w_edges, w_gate, w_out, mrow, mcol, out,
+    held, lwide, rwide, left, right, w2wide, w2, wq, wout, lbuf, rbuf, lt, prod,
+    z_opp, z_side, in_half, in_side, own, fbuf, wide, wfull,
+    updated, normed, gate, outgoing, edges, tri, back, tile, landed,
+    s_x, s_f, r_f, s_w, r_w, s_l1, r_l1, s_r1, r_r1, s_l2, r_l2, s_r2, r_r2, s_c, r_c,
+    s_h, r_h, s_z, r_z, s_e, r_e, s_t, r_t, s_o, r_o,
 ):
     y, z, x, k = position()
     feature_z, feature_k = (z // 2) * 2 + x % 2, x // 2
@@ -64,7 +64,6 @@
     ya, yb, yo = (y + 1) % 4, (y + 3) % 4, (y + 2) % 4
     xa, xb, xo = (x + 1) % 4, (x + 3) % 4, (x + 2) % 4
     za, zb, zo = (z + 1) % 4, (z + 3) % 4, (z + 2) % 4
-    up, down = at(y, za, x, k), at(y, zb, x, k)
     row_block = block_of(y, z, k)
 
     def load(g):
@@ -83,8 +82,8 @@
 
     lax.fori_loop(1, 128, greet, 0)
 
-    wl, wr = coef[:, :LAT], coef[:, LAT:]
-    wide_coef = jnp.concatenate([wl] * 4 + [wr] * 4, axis=1)
+    wl, wr = coef[:LAT], coef[LAT:]
+    wide_coef = jnp.concatenate([wl] * 4 + [wr] * 4, axis=0).T
     column_sum = jnp.sum(wide_coef.astype(F32), 0, keepdims=True)
     mask_columns = msa_mask[...].astype(F32).T
     lane_part = lax.broadcasted_iota(jnp.int32, (1, 128), 1) // LAT
@@ -112,6 +111,14 @@
     for d in range(LAT):
         right[d] = rwide[:, d, :].astype(BF16)
 
+    w2wide[...] = w_outer[...].astype(F32).reshape(LAT, LAT, C_Z)
+    for d in range(0, LAT, 4):
+        rows = jnp.concatenate([w2wide[:, d + h, :] for h in range(4)], axis=0)
+        w2[:, d * LAT : (d + 4) * LAT] = rows.T.astype(BF16)
+    wq[0:128] = w_edges[...]
+    wq[128:160] = w_gate[...]
+    wout[...] = w_out[...].T
+
     pl.semaphore_wait(barrier, 127)
 
     sends = []
@@ -124,16 +131,23 @@
     def left_block(o, h):
         return left.at[:, lanes((o // 2) * 4096 + h * 2048 + (o % 2) * 1024, 1024)]
 
+    def half_of(p):
+        return (z // 2 + 1 + p // 2) % 2
+
     for h in range(2):
-        target = lbuf.at[x, yk, :, h * 1024 : (h + 1) * 1024]
+        half = half_of(h * 2)
+        target = lbuf.at[x, yk, :, lanes(half * 1024, 1024)]
         for t in range(1, 8):
             o = (yk + t) % 8
-            push(left_block(o, h), target, s_l1.at[h, t], r_l1, at(o // 2, z, x, o % 2))
-        pltpu.make_async_copy(left_block(yk, h), target, r_l1).start()
-    for t in range(1, 4):
-        o = (x + t) % 4
-        push(right.at[:, :, lanes(o * 128, 128)], rbuf.at[:, x, yk], s_r1.at[t], r_r1, at(y, z, o, k))
-    pltpu.make_async_copy(right.at[:, :, lanes(x * 128, 128)], rbuf.at[:, x, yk], r_r1).start()
+            push(left_block(o, half), target, s_l1.at[h, t], r_l1.at[h], at(o // 2, z, x, o % 2))
+        pltpu.make_async_copy(left_block(yk, half), target, r_l1.at[h]).start()
+        for q in (h * 2, h * 2 + 1):
+            ds = pl.ds(q * 8, 8)
+            target_r = rbuf.at[ds, x, yk]
+            for t in range(1, 4):
+                o = (x + t) % 4
+                push(right.at[ds, :, lanes(o * 128, 128)], target_r, s_r1.at[q, t], r_r1.at[q], at(y, z, o, k))
+            pltpu.make_async_copy(right.at[ds, :, lanes(x * 128, 128)], target_r, r_r1.at[q]).start()
 
     for t in range(1, 4):
         push(wq, wfull.at[n], s_w.at[t], r_w, (w, (n + t) % 4))
@@ -145,21 +159,19 @@
             feat.at[:, :, t * 128 : (t + 1) * 128], fbuf.at[pl.ds(n * 32, 32)], s_f.at[t], r_f, (tw, tn)
         )
 
-    def half_of(p):
-        return (z // 2 + 1 + p // 2) % 2
-
     def left_part(slab, p):
         return lbuf.at[slab, (p % 2) * 4 : (p % 2) * 4 + 4, :, lanes(half_of(p) * 1024, 1024)]
 
     def right_part(yy, kk, q):
         return rbuf.at[q * 8 : (q + 1) * 8, :, yy * 2 + kk]
 
-    arrived(lbuf.at[x], r_l1)
-    for p in range(QUADS):
-        push(left_part(x, p), left_part(x, p), s_l2.at[0, p], r_l2.at[0, p], at(y, z, xa, k))
-        push(left_part(x, p), left_part(x, p), s_l2.at[1, p], r_l2.at[1, p], at(y, z, xb, k))
-    arrived(rbuf.at[:, :, yk], r_r1)
     for q in range(QUADS):
+        if q % 2 == 0:
+            arrived(lbuf.at[x, :, :, lanes(half_of(q) * 1024, 1024)], r_l1.at[q // 2])
+            for p in (q, q + 1):
+                push(left_part(x, p), left_part(x, p), s_l2.at[0, p], r_l2.at[0, p], at(y, z, xa, k))
+                push(left_part(x, p), left_part(x, p), s_l2.at[1, p], r_l2.at[1, p], at(y, z, xb, k))
+        arrived(rbuf.at[q * 8 : (q + 1) * 8, :, yk], r_r1.at[q])
         mine = right_part(y, k, q)
         push(mine, mine, s_r2.at[0, q], r_r2.at[0, q], at(ya, z, x, k))
         push(mine, mine, s_r2.at[1, q], r_r2.at[1, q], at(yb, z, x, k))
@@ -173,12 +185,11 @@
                 :, h * 128 : (h + 1) * 128
             ].reshape(16, 32, 128)
 
-    def products(half, first, last):
-        def step(t, carry):
-            product(half * 2 + t % 2, first + t // 2)
-            return carry
-
-        lax.fori_loop(0, (last - first) * 2, step, 0)
+    def products(half, q):
+        lax.fori_loop(0, 2, lambda t, c: (product(half * 2 + t, q), c)[1], 0)
+
+    def group_products(a):
+        lax.fori_loop(0, 4, lambda q, c: (product(a, q), c)[1], 0)
 
     def means(a, part, store):
         rows = [prod[a * 16 + part * 8 + h] for h in range(8)]
@@ -219,9 +230,7 @@
             for side, src in ((0, y), (1, yb), (2, ya), (3, yo)):
                 arrived(right_part(src, 1 - k, q), r_c.at[side, q])
             if q < QUADS - 1:
-                products(half_of(0), q, q + 1)
-                if q == QUADS - 2:
-                    products(half_of(2), 0, q + 1)
+                products(half_of(0), q)
 
     for t in range(4):
         tw, tn, copy = feature_copy(t)
@@ -234,83 +243,106 @@
         def _():
             pltpu.make_async_copy(feat.at[:, :, t * 128 : (t + 1) * 128], fbuf.at[pl.ds(n * 32, 32)], r_f).start()
 
+    def beyond(side):
+        return (z + 1 + side * 2) % 4
+
     def store_opp(i, value):
         z_opp[i] = value.astype(BF16)
 
     def store_own(i, value):
         own[i] = value
 
-    def store_up(i, value):
-        z_up[i] = value.astype(BF16)
-
-    def store_up_sum(i, value):
-        z_up[i] = (value + in_a[i].astype(F32)).astype(BF16)
-
-    def store_down(i, value):
-        z_dn[i] = value.astype(BF16)
-
-    def store_down_sum(i, value):
-        z_dn[i] = (value + in_b[i - 8].astype(F32)).astype(BF16)
+    def send_side(side, part, turn, store):
+        means(beyond(side), part, store)
+        rows = pl.ds(pl.multiple_of(part * 8, 8), 8)
+        push(
+            z_side.at[side, rows], in_side.at[side, rows],
+            s_z.at[side, turn], r_z.at[side, turn], at(y, beyond(side), x, k),
+        )
+
+    def send_early(side):
+        def store(i, value):
+            z_side[side, i] = value.astype(BF16)
+
+        send_side(side, 1 - side, 0, store)
+
+    def send_late(side):
+        def store(i, value):
+            z_side[side, i] = (value + in_half[side, i - side * 8].astype(F32)).astype(BF16)
+
+        arrived(in_half.at[side], r_h.at[side])
+        send_side(side, side, 1, store)
 
     product(zo, 3)
-    means(zo, 0, store_opp)
-    push(z_opp.at[0:8], in_a, s_z.at[0], r_z.at[0], up)
-    means(zo, 1, store_opp)
-    push(z_opp.at[8:16], in_b, s_z.at[1], r_z.at[1], down)
-    product(za, 3)
-    means(za, 1, store_up)
-    push(z_up.at[8:16], in_p.at[8:16], s_z.at[3], r_z.at[3], up)
-    product(zb, 3)
-    means(zb, 0, store_down)
-    push(z_dn.at[0:8], in_m.at[0:8], s_z.at[5], r_z.at[5], down)
-    arrived(in_a, r_z.at[0])
-    means(za, 0, store_up_sum)
-    push(z_up.at[0:8], in_p.at[0:8], s_z.at[2], r_z.at[2], up)
-    arrived(in_b, r_z.at[1])
-    means(zb, 1, store_down_sum)
-    push(z_dn.at[8:16], in_m.at[8:16], s_z.at[4], r_z.at[4], down)
-    product(z, 3)
+    for side in range(2):
+        means(zo, side, store_opp)
+        push(
+            z_opp.at[side * 8 : side * 8 + 8], in_half.at[side],
+            s_h.at[side], r_h.at[side], at(y, beyond(side), x, k),
+        )
+    far = 1 - z % 2
+    product(beyond(far), 3)
+    send_early(far)
+    group_products(beyond(1 - far))
+    send_early(1 - far)
+    group_products(z)
+    send_late(0)
+    send_late(1)
     for part in range(2):
         means(z, part, store_own)
 
     arrived(fbuf, r_f)
     wide[0] = fbuf[...].astype(F32)
+    for i in range(ROWS):
+        own[i] = own[i] + wide[0, :, i, :]
     arrived(wfull, r_w)
-    weights = wfull[...].reshape(640, C_Z)
-    col_on = mcol[pl.ds(x, 1), :]
-    arrived(in_p.at[8:16], r_z.at[3])
-    arrived(in_m.at[0:8], r_z.at[5])
-    arrived(in_p.at[0:8], r_z.at[2])
-    arrived(in_m.at[8:16], r_z.at[4])
+    col_on = mcol[pl.ds(x, 1), :].astype(F32)
+    for side in range(2):
+        for turn in range(2):
+            part = (1 - side) if turn == 0 else side
+            arrived(in_side.at[side, part * 8 : part * 8 + 8], r_z.at[side, turn])
     for i in range(ROWS):
-        total = own[i] + in_p[i].astype(F32) + in_m[i].astype(F32)
-        updated[i] = (wide[0, :, i, :] + total).astype(BF16)
-    for i in range(ROWS):
-        u = updated[i].astype(F32)
+        total = (own[i] + in_side[0, i].astype(F32) + in_side[1, i].astype(F32)).astype(BF16)
+        updated[i] = total
+        u = total.astype(F32)
         center = jnp.sum(u, 0, keepdims=True) * (1.0 / C_Z)
         spread = jnp.sum(u * u, 0, keepdims=True) * (1.0 / C_Z) - center * center
-        normed = ((u - center) * lax.rsqrt(spread + EPS)).astype(BF16)
-        proj = jnp.dot(weights, normed, preferred_element_type=F32)
-        on = col_on * mrow[row_block * ROWS + i].astype(F32)
-        for c in range(4):
-            base = c * 160
-            wide[0, c * 32 : (c + 1) * 32, i, :] = (
-                jax.nn.sigmoid(proj[base : base + 32]) * proj[base + 32 : base + 64] * on
-            )
-            wide[1, c * 32 : (c + 1) * 32, i, :] = (
-                jax.nn.sigmoid(proj[base + 64 : base + 96]) * proj[base + 96 : base + 128] * on
-            )
-            gate[i, c * 32 : (c + 1) * 32, :] = proj[base + 128 : base + 160]
-    for h in range(2):
-        outgoing[:, h] = wide[h].astype(BF16)
-
-    def send_edges(t, carry):
-        o = (me + t * 37) % 128
-        remote(outgoing.at[o], edges.at[:, x, row_block], s_e, r_e, (o // 4, o % 4)).start()
+        normed[i] = ((u - center) * lax.rsqrt(spread + EPS)).astype(BF16)
+
+    def edge_quarter(t, carry):
+        c = jnp.where(t == 3, y, (y + jnp.where(t == 0, 1, jnp.where(t == 1, 3, 2))) % 4)
+        span = pl.ds(c * 32, 32)
+        weights = wfull[c]
+        for g in range(4):
+            four = jnp.concatenate([normed[g * 4 + h] for h in range(4)], axis=1)
+            proj = jnp.dot(weights, four, preferred_element_type=F32)
+            for h in range(4):
+                i = g * 4 + h
+                p = proj[:, h * 128 : (h + 1) * 128]
+                on = col_on * mrow[row_block * ROWS + i].astype(F32)
+                wide[0, span, i, :] = jax.nn.sigmoid(p[0:32]) * p[32:64] * on
+                wide[1, span, i, :] = jax.nn.sigmoid(p[64:96]) * p[96:128] * on
+                gate[i, span, :] = p[128:160]
+        for h in range(2):
+            outgoing[span, h] = wide[h, span].astype(BF16)
+
+        def send_edges(t, carry):
+            o = c * 32 + (me + t * 11) % 32
+
+            @pl.when(o != me)
+            def _():
+                remote(outgoing.at[o], edges.at[:, x, row_block], s_e, r_e, (o // 4, o % 4)).start()
+
+            @pl.when(o == me)
+            def _():
+                pltpu.make_async_copy(outgoing.at[o], edges.at[:, x, row_block], r_e).start()
+
+            return carry
+
+        lax.fori_loop(0, 32, send_edges, 0)
         return carry
 
-    pltpu.make_async_copy(outgoing.at[me], edges.at[:, x, row_block], r_e).start()
-    lax.fori_loop(1, 128, send_edges, 0)
+    lax.fori_loop(0, 4, edge_quarter, 0)
     gate[...] = jax.nn.sigmoid(gate[...])
     arrived(edges, r_e)
 
@@ -345,20 +377,27 @@
         t = wide[0, :, i, :]
         center = jnp.sum(t, 0, keepdims=True) * (1.0 / C_Z)
         spread = jnp.sum(t * t, 0, keepdims=True) * (1.0 / C_Z) - center * center
-        normed = ((t - center) * lax.rsqrt(spread + EPS)).astype(BF16)
-        result = jnp.dot(wout[...], normed, preferred_element_type=F32)
-        wide[1, :, i, :] = updated[i].astype(F32) + gate[i] * result
-    tile[...] = wide[1].astype(BF16)
+        normed[i] = ((t - center) * lax.rsqrt(spread + EPS)).astype(BF16)
 
     def out_parts(t):
-        q = (x + t) % 4
+        q = (x + (1, 3, 2, 0)[t]) % 4
         part = tile.at[pl.ds(q * 32, 32)]
         place = landed.at[:, :, lanes(x * 128, 128)]
         away = (row_block != w) | (n != q)
-        return away, part, place, remote(part, place, s_o.at[t], r_o, (row_block, q))
+        return q, away, part, place, remote(part, place, s_o.at[t], r_o, (row_block, q))
 
     for t in range(4):
-        away, part, place, copy = out_parts(t)
+        q, away, part, place, copy = out_parts(t)
+        span = pl.ds(pl.multiple_of(q * 32, 32), 32)
+        for g in range(2):
+            eight = jnp.concatenate([normed[g * 8 + h] for h in range(8)], axis=1)
+            result = jnp.dot(wout[span, :], eight, preferred_element_type=F32)
+            for h in range(8):
+                i = g * 8 + h
+                wide[1, span, i, :] = (
+                    updated[i, span, :].astype(F32) + gate[i, span, :] * result[:, h * 128 : (h + 1) * 128]
+                )
+        tile[span] = wide[1, span].astype(BF16)
 
         @pl.when(away)
         def _():
@@ -374,7 +413,7 @@
     arrived(outgoing.at[0:127], s_e)
     arrived(back.at[0:127], s_t)
     for t in range(4):
-        away, part, place, copy = out_parts(t)
+        q, away, part, place, copy = out_parts(t)
 
         @pl.when(away)
         def _():
@@ -390,7 +429,7 @@
             copy.wait_send()
 
 
-def call(msa, msa_mask, feat, coef, w2, wq, wout, mrow, mcol):
+def call(*args):
     dma = pltpu.SemaphoreType.DMA
     vmem = pl.BlockSpec(memory_space=pltpu.VMEM)
     pair = pltpu.VMEM((ROWS, C_Z, 128), BF16)
@@ -399,7 +438,7 @@
         name="evoformer",
         out_shape=jax.ShapeDtypeStruct((32, ROWS, RES), BF16),
         in_specs=[pl.BlockSpec(memory_space=pl.ANY)]
-        + [vmem] * 6
+        + [vmem] * 7
         + [pl.BlockSpec(memory_space=pltpu.SMEM), vmem],
         out_specs=vmem,
         scratch_shapes=[
@@ -408,18 +447,23 @@
             pltpu.VMEM((16, LAT, RES), F32),
             pltpu.VMEM((16, RES * LAT), BF16),
             pltpu.VMEM((LAT, 16, RES), BF16),
+            pltpu.VMEM((LAT, LAT, C_Z), F32),
+            pltpu.VMEM((C_Z, LAT * LAT), BF16),
+            pltpu.VMEM((160, C_Z), BF16),
+            pltpu.VMEM((C_Z, C_Z), BF16),
             pltpu.VMEM((4, 8, 16, 2048), BF16),
             pltpu.VMEM((LAT, 4, 8, 16, 128), BF16),
             pltpu.VMEM((4, 512, 512), BF16),
             pltpu.VMEM((64, LAT * LAT, 128), BF16),
-            pair, pair, pair,
-            pltpu.VMEM((8, C_Z, 128), BF16),
-            pltpu.VMEM((8, C_Z, 128), BF16),
-            pair, pair,
+            pair,
+            pltpu.VMEM((2, ROWS, C_Z, 128), BF16),
+            pltpu.VMEM((2, 8, C_Z, 128), BF16),
+            pltpu.VMEM((2, ROWS, C_Z, 128), BF16),
             pltpu.VMEM((ROWS, C_Z, 128), F32),
             pltpu.VMEM((C_Z, ROWS, 128), BF16),
             pltpu.VMEM((2, C_Z, ROWS, 128), F32),
             pltpu.VMEM((4, 160, C_Z), BF16),
+            pair,
             pair,
             pltpu.VMEM((ROWS, C_Z, 128), F32),
             pltpu.VMEM((C_Z, 2, ROWS, 128), BF16),
@@ -430,16 +474,17 @@
             pltpu.VMEM((32, ROWS, RES), BF16),
             dma((4,)),
             dma((4,)), dma, dma((4,)), dma,
-            dma((2, 8)), dma, dma((4,)), dma,
+            dma((2, 8)), dma((2,)), dma((4, 4)), dma((4,)),
             dma((3, 4)), dma((3, 4)), dma((3, 4)), dma((3, 4)),
-            dma((4, 4)), dma((4, 4)), dma((6,)), dma((6,)),
+            dma((4, 4)), dma((4, 4)),
+            dma((2,)), dma((2,)), dma((2, 2)), dma((2, 2)),
             dma, dma, dma, dma, dma((4,)), dma,
         ],
         compiler_params=pltpu.CompilerParams(
-            collective_id=0, has_side_effects=True, vmem_limit_bytes=56 * 2**20
+            collective_id=0, has_side_effects=True, vmem_limit_bytes=52 * 2**20
         ),
         cost_estimate=pl.CostEstimate(flops=12 * 10**9, bytes_accessed=8 * 2**20, transcendentals=10**6),
-    )(msa, msa_mask, feat, coef, w2, wq, wout, mrow, mcol)
+    )(*args)
 
 
 def body(
@@ -453,13 +498,11 @@
     triangle_gate_weight,
     triangle_output_weight,
 ):
-    w2 = jnp.transpose(outer_output_weight.reshape(LAT, LAT, C_Z), (2, 1, 0)).reshape(C_Z, LAT * LAT)
-    wq = jnp.concatenate([triangle_input_weight, triangle_gate_weight[None]], 0)
-    wq = jnp.transpose(wq, (0, 2, 1)).reshape(160, C_Z)
+    edge_weights = jnp.transpose(triangle_input_weight, (0, 2, 1)).reshape(C_Z, C_Z)
     return call(
-        homolog_embedding, alignment_mask, pairwise_features, left_right_coefficients,
-        w2, wq, triangle_output_weight.T,
-        residue_validity_mask, residue_validity_mask.astype(F32).reshape(4, 128),
+        homolog_embedding, alignment_mask, pairwise_features, left_right_coefficients.T,
+        outer_output_weight, edge_weights, triangle_gate_weight.T, triangle_output_weight,
+        residue_validity_mask, residue_validity_mask.reshape(4, 128),
     )
 
 

time: 139 us -> 127 us (0.914)
  Pallas kernels: 129 us -> 119 us
  other arithmetic: 2.64 us -> 0 us
    pallas_call x1, Pallas kernels: 129 us -> 119 us  [call(): pl.pallas_call(kernel, name='evoformer', out_shape=jax.ShapeDtypeStruct((...]
    unnamed x3 -> x17, local copies, waits for them, and re-layouts: 4.82 us -> 7.19 us
where the time goes in v3:
time: 127 us; the launch traced here: 126 us
  Pallas kernels  119 us (94%)
  local copies, waits for them, and re-layouts  7.19 us (6%)
    pallas_call x1, Pallas kernels, call(): pl.pallas_call(kernel, name='evoformer', out_shape=jax.ShapeDtypeStruct((...  119 us
    unnamed x17, local copies, waits for them, and re-layouts  7.19 us

profile of v3, /device:TPU:1, one launch (start us, length us, event | category | flops | bytes accessed | tf_op | source)
XLA Modules:
  0.0 125.9 jit_solution(13129614504082795822)
XLA Ops:
  0.0 0.0 copy-start
  0.0 1.0 copy-done
  1.0 0.0 copy-start.1
  1.0 0.9 copy-done.1
  2.0 0.0 copy-start.2
  2.0 0.8 copy-done.2
  2.8 0.0 copy-start.3
  2.8 0.8 copy-done.3
  3.5 0.0 copy-start.4
  3.5 0.8 copy-done.4
  4.3 0.0 copy-start.5
  4.3 0.8 copy-done.5
  5.0 0.0 copy-start.6
  5.0 0.7 copy-done.6
  5.7 0.0 copy-start.7
  5.7 0.7 copy-done.7
  6.4 118.7 %evoformer.1 = bf16[32,16,512]{2,1,0:T(8,128)(2,1)S(1)} custom-call(bf16[16,512,256]{2,1,0:T(8,128)(2,1)} %msa.1, s32[16,512]{1,0:T(8,128)S(1)} %copy-done.2, bf16[32,16,512]{2,1,0:T(8,128)(2,1)S(1)} %copy-done, bf16[64,256]{1,0:T(8,128)(2,1)S(1)} %bitcast.6, bf16[1024,128]{1,0:T(8,128)(2,1)S(1)} %copy-done.1, bf16[128,128]{1,0:T(8,128)(2,1)S(1)} %bitcast.7, ...), custom_call_target="tpu_custom_call" | custom-call | flops 12000000000 | bytes 8388608 | tf_op jit(solution)/shard_map/evoformer/pallas_call | solution.py:436
  125.1 0.8 copy.11
Async XLA Ops:
  0.0 1.0 copy-start
  1.0 0.9 copy-start.1
  2.0 0.8 copy-start.2
  2.8 0.8 copy-start.3
  3.5 0.8 copy-start.4
  4.3 0.8 copy-start.5
  5.0 0.7 copy-start.6
  5.7 0.7 copy-start.7

commit v4 on v3

--- a/solution.py
+++ b/solution.py
@@ -26,8 +26,12 @@
     return y * 8 + (z // 2) * 4 + x, (z % 2) * 2 + k
 
 
-def block_of(y, z, k):
-    return y * 8 + (z // 2) * 4 + k * 2 + z % 2
+def group_of(z, x):
+    return (z // 2) * 2 + (z + x) % 2
+
+
+def block_of(y, z, x, k):
+    return y * 8 + (z // 2) * 4 + k * 2 + (z + x) % 2
 
 
 def remote(src, dst, send, recv, device):
@@ -49,29 +53,47 @@
 
 
 def kernel(
-    msa, msa_mask, feat, coef, w_outer, w_edges, w_gate, w_out, mrow, mcol, out,
+    msa, msa_mask_hbm, feat, coef_hbm, w_outer_hbm, w_edges, w_gate, w_out_hbm, mrow, mcol_hbm, out,
+    msa_mask, coef, w_outer, w_out, mcol,
     held, lwide, rwide, left, right, w2wide, w2, wq, wout, lbuf, rbuf, lt, prod,
     z_opp, z_side, in_half, in_side, own, fbuf, wide, wfull,
     updated, normed, gate, outgoing, edges, tri, back, tile, landed,
-    s_x, s_f, r_f, s_w, r_w, s_l1, r_l1, s_r1, r_r1, s_l2, r_l2, s_r2, r_r2, s_c, r_c,
+    s_x, s_i, s_f, r_f, s_w, r_w, s_l1, r_l1, s_r1, r_r1, s_l2, r_l2, s_r2, r_r2, s_c, r_c,
     s_h, r_h, s_z, r_z, s_e, r_e, s_t, r_t, s_o, r_o,
 ):
     y, z, x, k = position()
-    feature_z, feature_k = (z // 2) * 2 + x % 2, x // 2
     w, n = at(y, z, x, k)
     me = w * 4 + n
     yk = y * 2 + k
     ya, yb, yo = (y + 1) % 4, (y + 3) % 4, (y + 2) % 4
     xa, xb, xo = (x + 1) % 4, (x + 3) % 4, (x + 2) % 4
     za, zb, zo = (z + 1) % 4, (z + 3) % 4, (z + 2) % 4
-    row_block = block_of(y, z, k)
+    row_block = block_of(y, z, x, k)
 
     def load(g):
         part = pl.ds(g * 4, 4)
         return pltpu.make_async_copy(msa.at[part], held.at[part], s_x.at[g])
 
+    small = [
+        pltpu.make_async_copy(src, dst, s_i.at[t])
+        for t, (src, dst) in enumerate(
+            (
+                (coef_hbm, coef),
+                (msa_mask_hbm, msa_mask),
+                (w_outer_hbm, w_outer),
+                (w_out_hbm, w_out),
+                (mcol_hbm, mcol),
+                (w_edges, wq.at[0:128]),
+                (w_gate, wq.at[128:160]),
+            )
+        )
+    ]
+    small[0].start()
+    small[1].start()
     for g in range(4):
         load(g).start()
+    for copy in small[2:]:
+        copy.start()
 
     barrier = pltpu.get_barrier_semaphore()
 
@@ -82,6 +104,8 @@
 
     lax.fori_loop(1, 128, greet, 0)
 
+    small[0].wait()
+    small[1].wait()
     wl, wr = coef[:LAT], coef[LAT:]
     wide_coef = jnp.concatenate([wl] * 4 + [wr] * 4, axis=0).T
     column_sum = jnp.sum(wide_coef.astype(F32), 0, keepdims=True)
@@ -111,12 +135,12 @@
     for d in range(LAT):
         right[d] = rwide[:, d, :].astype(BF16)
 
+    for copy in small[2:]:
+        copy.wait()
     w2wide[...] = w_outer[...].astype(F32).reshape(LAT, LAT, C_Z)
     for d in range(0, LAT, 4):
         rows = jnp.concatenate([w2wide[:, d + h, :] for h in range(4)], axis=0)
         w2[:, d * LAT : (d + 4) * LAT] = rows.T.astype(BF16)
-    wq[0:128] = w_edges[...]
-    wq[128:160] = w_gate[...]
     wout[...] = w_out[...].T
 
     pl.semaphore_wait(barrier, 127)
@@ -154,7 +178,7 @@
     pltpu.make_async_copy(wq, wfull.at[n], r_w).start()
 
     def feature_copy(t):
-        tw, tn = at(y, feature_z, t, feature_k)
+        tw, tn = at(y, (z // 2) * 2 + (x + t) % 2, t, x // 2)
         return tw, tn, remote(
             feat.at[:, :, t * 128 : (t + 1) * 128], fbuf.at[pl.ds(n * 32, 32)], s_f.at[t], r_f, (tw, tn)
         )
@@ -165,17 +189,23 @@
     def right_part(yy, kk, q):
         return rbuf.at[q * 8 : (q + 1) * 8, :, yy * 2 + kk]
 
-    for q in range(QUADS):
-        if q % 2 == 0:
-            arrived(lbuf.at[x, :, :, lanes(half_of(q) * 1024, 1024)], r_l1.at[q // 2])
-            for p in (q, q + 1):
-                push(left_part(x, p), left_part(x, p), s_l2.at[0, p], r_l2.at[0, p], at(y, z, xa, k))
-                push(left_part(x, p), left_part(x, p), s_l2.at[1, p], r_l2.at[1, p], at(y, z, xb, k))
+    def own_left(p):
+        if p % 2 == 0:
+            arrived(lbuf.at[x, :, :, lanes(half_of(p) * 1024, 1024)], r_l1.at[p // 2])
+        push(left_part(x, p), left_part(x, p), s_l2.at[0, p], r_l2.at[0, p], at(y, z, xa, k))
+        push(left_part(x, p), left_part(x, p), s_l2.at[1, p], r_l2.at[1, p], at(y, z, xb, k))
+
+    def own_right(q):
         arrived(rbuf.at[q * 8 : (q + 1) * 8, :, yk], r_r1.at[q])
         mine = right_part(y, k, q)
         push(mine, mine, s_r2.at[0, q], r_r2.at[0, q], at(ya, z, x, k))
         push(mine, mine, s_r2.at[1, q], r_r2.at[1, q], at(yb, z, x, k))
         push(mine, mine, s_c.at[0, q], r_c.at[0, q], at(y, z, x, 1 - k))
+
+    own_left(0)
+    own_right(0)
+    own_left(1)
+    own_right(1)
 
     def product(a, q):
         parts = [rbuf[q * 8 + h].reshape(512, 128) for h in range(8)]
@@ -212,6 +242,9 @@
                 arrived(part, r_l2.at[0 if upward else 1, p])
                 if upward == (p % 2 == 0):
                     push(part, part, s_l2.at[2, p], r_l2.at[2, p], at(y, z, xa if upward else xb, k))
+            if step + 2 < QUADS:
+                own_left(step + 2)
+                own_right(step + 2)
         if 0 <= step - 1 < QUADS:
             p = q = step - 1
             part = right_part(yo, k, q)
@@ -253,7 +286,7 @@
         own[i] = value
 
     def send_side(side, part, turn, store):
-        means(beyond(side), part, store)
+        means(group_of(beyond(side), x), part, store)
         rows = pl.ds(pl.multiple_of(part * 8, 8), 8)
         push(
             z_side.at[side, rows], in_side.at[side, rows],
@@ -273,23 +306,23 @@
         arrived(in_half.at[side], r_h.at[side])
         send_side(side, side, 1, store)
 
-    product(zo, 3)
+    product(group_of(zo, x), 3)
     for side in range(2):
-        means(zo, side, store_opp)
+        means(group_of(zo, x), side, store_opp)
         push(
             z_opp.at[side * 8 : side * 8 + 8], in_half.at[side],
             s_h.at[side], r_h.at[side], at(y, beyond(side), x, k),
         )
     far = 1 - z % 2
-    product(beyond(far), 3)
+    product(group_of(beyond(far), x), 3)
     send_early(far)
-    group_products(beyond(1 - far))
+    group_products(group_of(beyond(1 - far), x))
     send_early(1 - far)
-    group_products(z)
+    group_products(group_of(z, x))
     send_late(0)
     send_late(1)
     for part in range(2):
-        means(z, part, store_own)
+        means(group_of(z, x), part, store_own)
 
     arrived(fbuf, r_f)
     wide[0] = fbuf[...].astype(F32)
@@ -357,7 +390,7 @@
 
         def send_back(t, carry):
             r = (row_block + t * 11) % 32
-            tw, tn = at(r // 8, ((r // 4) % 2) * 2 + r % 2, b, (r // 2) % 2)
+            tw, tn = at(r // 8, ((r // 4) % 2) * 2 + (r + b) % 2, b, (r // 2) % 2)
 
             @pl.when((tw != w) | (tn != n))
             def _():
@@ -432,16 +465,20 @@
 def call(*args):
     dma = pltpu.SemaphoreType.DMA
     vmem = pl.BlockSpec(memory_space=pltpu.VMEM)
+    hbm = pl.BlockSpec(memory_space=pltpu.HBM)
     pair = pltpu.VMEM((ROWS, C_Z, 128), BF16)
     return pl.pallas_call(
         kernel,
         name="evoformer",
         out_shape=jax.ShapeDtypeStruct((32, ROWS, RES), BF16),
-        in_specs=[pl.BlockSpec(memory_space=pl.ANY)]
-        + [vmem] * 7
-        + [pl.BlockSpec(memory_space=pltpu.SMEM), vmem],
+        in_specs=[hbm] * 8 + [pl.BlockSpec(memory_space=pltpu.SMEM), hbm],
         out_specs=vmem,
         scratch_shapes=[
+            pltpu.VMEM((16, RES), jnp.int32),
+            pltpu.VMEM((2 * LAT, 256), BF16),
+            pltpu.VMEM((LAT * LAT, C_Z), BF16),
+            pltpu.VMEM((C_Z, C_Z), BF16),
+            pltpu.VMEM((4, 128), jnp.int32),
             pltpu.VMEM((16, RES, 256), BF16),
             pltpu.VMEM((16, 128, 128), F32),
             pltpu.VMEM((16, LAT, RES), F32),
@@ -472,7 +509,7 @@
             pltpu.VMEM((C_Z, ROWS, 128), BF16),
             pltpu.VMEM((C_Z, ROWS, 128), BF16),
             pltpu.VMEM((32, ROWS, RES), BF16),
-            dma((4,)),
+            dma((4,)), dma((7,)),
             dma((4,)), dma, dma((4,)), dma,
             dma((2, 8)), dma((2,)), dma((4, 4)), dma((4,)),
             dma((3, 4)), dma((3, 4)), dma((3, 4)), dma((3, 4)),
@@ -481,7 +518,7 @@
             dma, dma, dma, dma, dma((4,)), dma,
         ],
         compiler_params=pltpu.CompilerParams(
-            collective_id=0, has_side_effects=True, vmem_limit_bytes=52 * 2**20
+            collective_id=0, has_side_effects=True, vmem_limit_bytes=60 * 2**20
         ),
         cost_estimate=pl.CostEstimate(flops=12 * 10**9, bytes_accessed=8 * 2**20, transcendentals=10**6),
     )(*args)

time: 127 us -> 116 us (0.913)
  local copies, waits for them, and re-layouts: 7.19 us -> 1.87 us
  Pallas kernels: 119 us -> 114 us
    unnamed x17 -> x1, local copies, waits for them, and re-layouts: 7.19 us -> 1.87 us
    pallas_call x1, Pallas kernels: 119 us -> 114 us  [call(): pl.pallas_call(kernel, name='evoformer', out_shape=jax.ShapeDtypeStruct((...]
where the time goes in v4:
time: 116 us
  Pallas kernels  114 us (98%)
  local copies, waits for them, and re-layouts  1.87 us (2%)
    pallas_call x1, Pallas kernels, call(): pl.pallas_call(kernel, name='evoformer', out_shape=jax.ShapeDtypeStruct((...  114 us

profile of v4, /device:TPU:1, one launch (start us, length us, event | category | flops | bytes accessed | tf_op | source)
XLA Modules:
  0.0 115.9 jit_solution(15569273662070483224)
XLA Ops:
  0.0 114.0 %evoformer.1 = bf16[32,16,512]{2,1,0:T(8,128)(2,1)} custom-call(bf16[16,512,256]{2,1,0:T(8,128)(2,1)} %msa.1, s32[16,512]{1,0:T(8,128)} %msa_mask_hbm.1, bf16[32,16,512]{2,1,0:T(8,128)(2,1)} %feat.1, bf16[64,256]{1,0:T(8,128)(2,1)} %bitcast.6, bf16[1024,128]{1,0:T(8,128)(2,1)} %w_outer_hbm.1, bf16[128,128]{1,0:T(8,128)(2,1)} %bitcast.7, ...), custom_call_target="tpu_custom_call" | custom-call | flops 12000000000 | bytes 8388608 | tf_op jit(solution)/shard_map/evoformer/pallas_call | solution.py:470
  114.0 1.9 %copy.11 = bf16[32,16,512]{2,1,0:T(8,128)(2,1)} copy(bf16[32,16,512]{2,1,0:T(8,128)(2,1)} %evoformer.1) | data formatting | bytes 1048576

commit v5 on v4

--- a/solution.py
+++ b/solution.py
@@ -56,9 +56,9 @@
     msa, msa_mask_hbm, feat, coef_hbm, w_outer_hbm, w_edges, w_gate, w_out_hbm, mrow, mcol_hbm, out,
     msa_mask, coef, w_outer, w_out, mcol,
     held, lwide, rwide, left, right, w2wide, w2, wq, wout, lbuf, rbuf, lt, prod,
-    z_opp, z_side, in_half, in_side, own, fbuf, wide, wfull,
-    updated, normed, gate, outgoing, edges, tri, back, tile, landed,
-    s_x, s_i, s_f, r_f, s_w, r_w, s_l1, r_l1, s_r1, r_r1, s_l2, r_l2, s_r2, r_r2, s_c, r_c,
+    z_opp, z_side, in_half, in_side, own, fhalf, fbuf, wide, wfull,
+    updated, normed, gate, outgoing, edges, tri, back, tile,
+    s_x, s_i, s_g, r_g, s_f, r_f, s_w, r_w, s_l1, r_l1, s_r1, r_r1, s_l2, r_l2, s_r2, r_r2, s_c, r_c,
     s_h, r_h, s_z, r_z, s_e, r_e, s_t, r_t, s_o, r_o,
 ):
     y, z, x, k = position()
@@ -97,12 +97,11 @@
 
     barrier = pltpu.get_barrier_semaphore()
 
-    def greet(t, carry):
-        o = (me + t) % 128
-        signal(barrier, (o // 4, o % 4))
-        return carry
-
-    lax.fori_loop(1, 128, greet, 0)
+    ws, ns = [(w + t) % 32 for t in range(32)], [(n + t) % 4 for t in range(4)]
+
+    def greet(first, last):
+        for t in range(first, last):
+            signal(barrier, (ws[t // 4], ns[t % 4]))
 
     small[0].wait()
     small[1].wait()
@@ -116,6 +115,8 @@
         packed = jnp.zeros((RES, 128), F32)
         for h in range(4):
             s = g * 4 + h
+            if g == 0:
+                greet(max(h * 32, 1), h * 32 + 32)
             values = held[s]
             v = values.astype(F32)
             center = jnp.sum(v, 1, keepdims=True) * (1.0 / 256)
@@ -135,14 +136,6 @@
     for d in range(LAT):
         right[d] = rwide[:, d, :].astype(BF16)
 
-    for copy in small[2:]:
-        copy.wait()
-    w2wide[...] = w_outer[...].astype(F32).reshape(LAT, LAT, C_Z)
-    for d in range(0, LAT, 4):
-        rows = jnp.concatenate([w2wide[:, d + h, :] for h in range(4)], axis=0)
-        w2[:, d * LAT : (d + 4) * LAT] = rows.T.astype(BF16)
-    wout[...] = w_out[...].T
-
     pl.semaphore_wait(barrier, 127)
 
     sends = []
@@ -173,15 +166,35 @@
                 push(right.at[ds, :, lanes(o * 128, 128)], target_r, s_r1.at[q, t], r_r1.at[q], at(y, z, o, k))
             pltpu.make_async_copy(right.at[ds, :, lanes(x * 128, 128)], target_r, r_r1.at[q]).start()
 
+    for copy in small[2:]:
+        copy.wait()
+    w2wide[...] = w_outer[...].astype(F32).reshape(LAT, LAT, C_Z)
+    for d in range(0, LAT, 4):
+        rows = jnp.concatenate([w2wide[:, d + h, :] for h in range(4)], axis=0)
+        w2[:, d * LAT : (d + 4) * LAT] = rows.T.astype(BF16)
+    wout[...] = w_out[...].T
+
     for t in range(1, 4):
         push(wq, wfull.at[n], s_w.at[t], r_w, (w, (n + t) % 4))
     pltpu.make_async_copy(wq, wfull.at[n], r_w).start()
 
-    def feature_copy(t):
-        tw, tn = at(y, (z // 2) * 2 + (x + t) % 2, t, x // 2)
-        return tw, tn, remote(
-            feat.at[:, :, t * 128 : (t + 1) * 128], fbuf.at[pl.ds(n * 32, 32)], s_f.at[t], r_f, (tw, tn)
-        )
+    zl = z % 2
+    partner = (1 - zl) * 2 + k
+    for t in range(2):
+        column = lanes(((x + 1 - zl + 2 * t) % 4) * 128, 128)
+        push(feat.at[:, :, column], fhalf.at[t], s_g.at[t], r_g, (w, partner))
+
+    def feature_copies(t):
+        xt = (x + zl + 2 * t) % 4
+        device = at(y, z, xt, x // 2)
+        legs = ((feat.at[:, :, lanes(xt * 128, 128)], n), (fhalf.at[t], partner))
+        places = [fbuf.at[pl.ds(pl.multiple_of(m * 32, 32), 32)] for _, m in legs]
+        stays = (t == 0) & (zl == 0) & (k == x // 2)
+        local = [pltpu.make_async_copy(src, dst, r_f) for (src, _), dst in zip(legs, places)]
+        away = [
+            remote(src, dst, s_f.at[t, h], r_f, device) for h, ((src, _), dst) in enumerate(zip(legs, places))
+        ]
+        return stays, local, away
 
     def left_part(slab, p):
         return lbuf.at[slab, (p % 2) * 4 : (p % 2) * 4 + 4, :, lanes(half_of(p) * 1024, 1024)]
@@ -255,9 +268,9 @@
                 half = half_of(p)
                 turned = lbuf[:, :, :, lanes(half * 1024, 1024)].reshape(512, 1024).T
                 for m in range(32):
-                    zl, i = m // 16, m % 16
-                    row = ((i % 8) * 4 + zl * 2 + i // 8) * 32
-                    lt[half * 2 + zl, i * 32 : (i + 1) * 32] = turned[row : row + 32]
+                    low, i = m // 16, m % 16
+                    row = ((i % 8) * 4 + low * 2 + i // 8) * 32
+                    lt[half * 2 + low, i * 32 : (i + 1) * 32] = turned[row : row + 32]
         if 0 <= step - 2:
             q = step - 2
             for side, src in ((0, y), (1, yb), (2, ya), (3, yo)):
@@ -265,16 +278,19 @@
             if q < QUADS - 1:
                 products(half_of(0), q)
 
-    for t in range(4):
-        tw, tn, copy = feature_copy(t)
-
-        @pl.when((tw != w) | (tn != n))
+    arrived(fhalf, r_g)
+    for t in range(2):
+        stays, local, away = feature_copies(t)
+
+        @pl.when(jnp.logical_not(stays))
         def _():
-            copy.start()
-
-        @pl.when((tw == w) & (tn == n))
+            for copy in away:
+                copy.start()
+
+        @pl.when(stays)
         def _():
-            pltpu.make_async_copy(feat.at[:, :, t * 128 : (t + 1) * 128], fbuf.at[pl.ds(n * 32, 32)], r_f).start()
+            for copy in local:
+                copy.start()
 
     def beyond(side):
         return (z + 1 + side * 2) % 4
@@ -342,10 +358,9 @@
         spread = jnp.sum(u * u, 0, keepdims=True) * (1.0 / C_Z) - center * center
         normed[i] = ((u - center) * lax.rsqrt(spread + EPS)).astype(BF16)
 
-    def edge_quarter(t, carry):
-        c = jnp.where(t == 3, y, (y + jnp.where(t == 0, 1, jnp.where(t == 1, 3, 2))) % 4)
+    def edge_quarter(c, first):
         span = pl.ds(c * 32, 32)
-        weights = wfull[c]
+        weights = wfull[c, 0:128]
         for g in range(4):
             four = jnp.concatenate([normed[g * 4 + h] for h in range(4)], axis=1)
             proj = jnp.dot(weights, four, preferred_element_type=F32)
@@ -355,31 +370,34 @@
                 on = col_on * mrow[row_block * ROWS + i].astype(F32)
                 wide[0, span, i, :] = jax.nn.sigmoid(p[0:32]) * p[32:64] * on
                 wide[1, span, i, :] = jax.nn.sigmoid(p[64:96]) * p[96:128] * on
-                gate[i, span, :] = p[128:160]
         for h in range(2):
             outgoing[span, h] = wide[h, span].astype(BF16)
 
-        def send_edges(t, carry):
-            o = c * 32 + (me + t * 11) % 32
-
-            @pl.when(o != me)
-            def _():
-                remote(outgoing.at[o], edges.at[:, x, row_block], s_e, r_e, (o // 4, o % 4)).start()
-
-            @pl.when(o == me)
-            def _():
-                pltpu.make_async_copy(outgoing.at[o], edges.at[:, x, row_block], r_e).start()
-
-            return carry
-
-        lax.fori_loop(0, 32, send_edges, 0)
+        for t in range(first, 32):
+            tw = c * 8 + lows[t // 4]
+            tn = ns[t % 4]
+            remote(outgoing.at[tw * 4 + tn], edges.at[:, x, row_block], s_e, r_e, (tw, tn)).start()
+
+    lows = [((w // 4 + t % 2) % 2) * 4 + (x + t // 2) % 4 for t in range(8)]
+
+    def far_quarter(t, carry):
+        edge_quarter((y + jnp.where(t == 0, 2, 2 * t - 1)) % 4, 0)
         return carry
 
-    lax.fori_loop(0, 4, edge_quarter, 0)
-    gate[...] = jax.nn.sigmoid(gate[...])
+    lax.fori_loop(0, 3, far_quarter, 0)
+    edge_quarter(y, 1)
+    pltpu.make_async_copy(outgoing.at[me], edges.at[:, x, row_block], r_e).start()
+    gate_weights = jnp.concatenate([wfull[c, 128:160] for c in range(4)], axis=0)
+    for g in range(4):
+        four = jnp.concatenate([normed[g * 4 + h] for h in range(4)], axis=1)
+        opened = jax.nn.sigmoid(jnp.dot(gate_weights, four, preferred_element_type=F32))
+        for h in range(4):
+            gate[g * 4 + h] = opened[:, h * 128 : (h + 1) * 128]
     arrived(edges, r_e)
 
     first = jnp.concatenate([edges[0, b].reshape(RES, 128) for b in range(4)], axis=1)
+    ys = [y, ya, yb, yo]
+    hs, ls, ks = [z // 2, 1 - z // 2], [z % 2, 1 - z % 2], [k, 1 - k]
     for q in (1, 3, 2, 0):
         b = (x + q) % 4
         second = jnp.concatenate(
@@ -388,21 +406,13 @@
         value = lax.dot_general(first, second, (((1,), (1,)), ((), ())), preferred_element_type=F32)
         tri[b] = value.astype(BF16).reshape(32, ROWS, 128)
 
-        def send_back(t, carry):
-            r = (row_block + t * 11) % 32
-            tw, tn = at(r // 8, ((r // 4) % 2) * 2 + (r + b) % 2, b, (r // 2) % 2)
-
-            @pl.when((tw != w) | (tn != n))
-            def _():
-                remote(tri.at[b, r], back.at[me], s_t, r_t, (tw, tn)).start()
-
-            @pl.when((tw == w) & (tn == n))
-            def _():
-                pltpu.make_async_copy(tri.at[b, r], back.at[me], r_t).start()
-
-            return carry
-
-        lax.fori_loop(0, 32, send_back, 0)
+        for t in range(32):
+            ty, th, tl, tk = ys[t % 4], hs[(t // 4) % 2], ls[(t // 8) % 2], ks[t // 16]
+            part = tri.at[b, ty * 8 + th * 4 + tk * 2 + (tl + b) % 2]
+            if t or q:
+                remote(part, back.at[me], s_t, r_t, (ty * 8 + th * 4 + b, tl * 2 + tk)).start()
+            else:
+                pltpu.make_async_copy(part, back.at[me], r_t).start()
 
     arrived(back, r_t)
     wide[0] = back[...].astype(F32)
@@ -415,7 +425,7 @@
     def out_parts(t):
         q = (x + (1, 3, 2, 0)[t]) % 4
         part = tile.at[pl.ds(q * 32, 32)]
-        place = landed.at[:, :, lanes(x * 128, 128)]
+        place = out.at[:, :, lanes(x * 128, 128)]
         away = (row_block != w) | (n != q)
         return q, away, part, place, remote(part, place, s_o.at[t], r_o, (row_block, q))
 
@@ -440,8 +450,7 @@
         def _():
             pltpu.make_async_copy(part, place, r_o).start()
 
-    arrived(landed, r_o)
-    out[...] = landed[...]
+    arrived(out, r_o)
 
     arrived(outgoing.at[0:127], s_e)
     arrived(back.at[0:127], s_t)
@@ -454,17 +463,17 @@
 
     for copy in sends:
         copy.wait_send()
-    for t in range(4):
-        tw, tn, copy = feature_copy(t)
-
-        @pl.when((tw != w) | (tn != n))
+    for t in range(2):
+        stays, local, away = feature_copies(t)
+
+        @pl.when(jnp.logical_not(stays))
         def _():
-            copy.wait_send()
+            for copy in away:
+                copy.wait_send()
 
 
 def call(*args):
     dma = pltpu.SemaphoreType.DMA
-    vmem = pl.BlockSpec(memory_space=pltpu.VMEM)
     hbm = pl.BlockSpec(memory_space=pltpu.HBM)
     pair = pltpu.VMEM((ROWS, C_Z, 128), BF16)
     return pl.pallas_call(
@@ -472,7 +481,7 @@
         name="evoformer",
         out_shape=jax.ShapeDtypeStruct((32, ROWS, RES), BF16),
         in_specs=[hbm] * 8 + [pl.BlockSpec(memory_space=pltpu.SMEM), hbm],
-        out_specs=vmem,
+        out_specs=hbm,
         scratch_shapes=[
             pltpu.VMEM((16, RES), jnp.int32),
             pltpu.VMEM((2 * LAT, 256), BF16),
@@ -497,6 +506,7 @@
             pltpu.VMEM((2, 8, C_Z, 128), BF16),
             pltpu.VMEM((2, ROWS, C_Z, 128), BF16),
             pltpu.VMEM((ROWS, C_Z, 128), F32),
+            pltpu.VMEM((2, 32, ROWS, 128), BF16),
             pltpu.VMEM((C_Z, ROWS, 128), BF16),
             pltpu.VMEM((2, C_Z, ROWS, 128), F32),
             pltpu.VMEM((4, 160, C_Z), BF16),
@@ -508,9 +518,8 @@
             pltpu.VMEM((4, 32, ROWS, 128), BF16),
             pltpu.VMEM((C_Z, ROWS, 128), BF16),
             pltpu.VMEM((C_Z, ROWS, 128), BF16),
-            pltpu.VMEM((32, ROWS, RES), BF16),
             dma((4,)), dma((7,)),
-            dma((4,)), dma, dma((4,)), dma,
+            dma((2,)), dma, dma((2, 2)), dma, dma((4,)), dma,
             dma((2, 8)), dma((2,)), dma((4, 4)), dma((4,)),
             dma((3, 4)), dma((3, 4)), dma((3, 4)), dma((3, 4)),
             dma((4, 4)), dma((4, 4)),

time: 116 us -> 108 us (0.931)
  Pallas kernels: 114 us -> 106 us
    pallas_call x1, Pallas kernels: 114 us -> 106 us  [call(): pl.pallas_call(kernel, name='evoformer', out_shape=jax.ShapeDtypeStruct((...]
where the time goes in v5:
time: 108 us; the launch traced here: 107 us
  Pallas kernels  106 us (98%)
  local copies, waits for them, and re-layouts  1.87 us (2%)
    pallas_call x1, Pallas kernels, call(): pl.pallas_call(kernel, name='evoformer', out_shape=jax.ShapeDtypeStruct((...  106 us

profile of v5, /device:TPU:1, one launch (start us, length us, event | category | flops | bytes accessed | tf_op | source)
XLA Modules:
  0.0 107.4 jit_solution(12581962826189369904)
XLA Ops:
  0.0 105.5 %evoformer.1 = bf16[32,16,512]{2,1,0:T(8,128)(2,1)} custom-call(bf16[16,512,256]{2,1,0:T(8,128)(2,1)} %msa.1, s32[16,512]{1,0:T(8,128)} %msa_mask_hbm.1, bf16[32,16,512]{2,1,0:T(8,128)(2,1)} %feat.1, bf16[64,256]{1,0:T(8,128)(2,1)} %bitcast.6, bf16[1024,128]{1,0:T(8,128)(2,1)} %w_outer_hbm.1, bf16[128,128]{1,0:T(8,128)(2,1)} %bitcast.7, ...), custom_call_target="tpu_custom_call" | custom-call | flops 12000000000 | bytes 8388608 | tf_op jit(solution)/shard_map/evoformer/pallas_call | solution.py:479
  105.5 1.9 %copy.11 = bf16[32,16,512]{2,1,0:T(8,128)(2,1)} copy(bf16[32,16,512]{2,1,0:T(8,128)(2,1)} %evoformer.1) | data formatting | bytes 1048576

commit v6 on v5

--- a/solution.py
+++ b/solution.py
@@ -103,6 +103,7 @@
         for t in range(first, last):
             signal(barrier, (ws[t // 4], ns[t % 4]))
 
+    greet(1, 128)
     small[0].wait()
     small[1].wait()
     wl, wr = coef[:LAT], coef[LAT:]
@@ -115,8 +116,6 @@
         packed = jnp.zeros((RES, 128), F32)
         for h in range(4):
             s = g * 4 + h
-            if g == 0:
-                greet(max(h * 32, 1), h * 32 + 32)
             values = held[s]
             v = values.astype(F32)
             center = jnp.sum(v, 1, keepdims=True) * (1.0 / 256)

time: 108 us -> 107 us (level)
  no operation moved by 1% of the time
where the time goes in v6:
time: 107 us; the launch traced here: 106 us
  Pallas kernels  105 us (98%)
  local copies, waits for them, and re-layouts  1.87 us (2%)
    pallas_call x1, Pallas kernels, call(): pl.pallas_call(kernel, name='evoformer', out_shape=jax.ShapeDtypeStruct((...  105 us

profile of v6, /device:TPU:1, one launch (start us, length us, event | category | flops | bytes accessed | tf_op | source)
XLA Modules:
  0.0 106.4 jit_solution(5493326579166892115)
XLA Ops:
  0.0 104.6 %evoformer.1 = bf16[32,16,512]{2,1,0:T(8,128)(2,1)} custom-call(bf16[16,512,256]{2,1,0:T(8,128)(2,1)} %msa.1, s32[16,512]{1,0:T(8,128)} %msa_mask_hbm.1, bf16[32,16,512]{2,1,0:T(8,128)(2,1)} %feat.1, bf16[64,256]{1,0:T(8,128)(2,1)} %bitcast.6, bf16[1024,128]{1,0:T(8,128)(2,1)} %w_outer_hbm.1, bf16[128,128]{1,0:T(8,128)(2,1)} %bitcast.7, ...), custom_call_target="tpu_custom_call" | custom-call | flops 12000000000 | bytes 8388608 | tf_op jit(solution)/shard_map/evoformer/pallas_call | solution.py:478
  104.6 1.9 %copy.11 = bf16[32,16,512]{2,1,0:T(8,128)(2,1)} copy(bf16[32,16,512]{2,1,0:T(8,128)(2,1)} %evoformer.1) | data formatting | bytes 1048576
